TPU v7x, 512 devices: a whole 4x8x8 slice. The times are simulated.
512 devices in a mesh: gx: 16 (over x, y_hi), gy: 32 (over z, y_lo, core).
Axes of the slice: x: 4, y: 8 (y_hi: 4, y_lo: 2; y = y_hi * 2 + y_lo), z: 8, core: 2. Of those that a mesh axis runs over, the one named last changes fastest.
Arguments:
- features: bfloat16 [128, 128, 18, 512], P('gx', 'gy'), may hold values from -6 to 6
- mode_weights: bfloat16 [64, 24, 2, 18, 18, 24], P('gy'), may hold values from -0.75 to 0.75
- point_weight: bfloat16 [18, 18], replicated, may hold values from -1.5 to 1.5
- bias_term: float32 [18], replicated, may hold values from -4 to 4
- conv_weight: bfloat16 [27, 18, 18], replicated, may hold values from -0.5 to 0.5
Outputs:
- updated: bfloat16 [128, 128, 18, 512], P('gx', 'gy')
All inputs are finite; a program needn't handle non-finite values.
Results may differ from a plain program's by a relative error of at most 0.0085.
Values may be sent and summed in bfloat16 or wider, within the bound.
A program may use at most 128 MiB of HBM per device.

v0:
```python
import math

import jax
import jax.numpy as jnp
from jax import lax
from jax.sharding import PartitionSpec as P

GRID_Z = 64
STEPS = 8
MZ = 16
MT = 4


def with_halo(block, sides, width):
    for axis, dim in sides:
        count = lax.axis_size(axis)
        forward = [(i, i + 1) for i in range(count - 1)]
        backward = [(target, source) for source, target in forward]
        low = lax.ppermute(
            lax.slice_in_dim(block, block.shape[dim] - width, None, axis=dim), axis, forward
        )
        high = lax.ppermute(lax.slice_in_dim(block, 0, width, axis=dim), axis, backward)
        block = jnp.concatenate([low, block, high], axis=dim)
    return block


def frequencies(number):
    places = jnp.arange(number, dtype=jnp.int32)
    return jnp.where(places < number // 2, places, places - number)


def phase_angles(number, positions, length):
    fraction = (
        jnp.mod(frequencies(number)[:, None] * positions[None, :], length).astype(jnp.float32)
        / length
    )
    return 2.0 * math.pi * fraction


def forward_table(number, positions, length):
    angles = phase_angles(number, positions, length).T
    cosine = jnp.cos(angles) / math.sqrt(length)
    sine_part = jnp.sin(angles) / math.sqrt(length)
    return jnp.stack(
        [jnp.stack([cosine, -sine_part], 1), jnp.stack([sine_part, cosine], 1)], 0
    ).astype(jnp.bfloat16)


def inverse_table(number, positions, length):
    angles = phase_angles(number, positions, length)
    cosine = jnp.cos(angles) / math.sqrt(number)
    sine_part = jnp.sin(angles) / math.sqrt(number)
    return jnp.stack(
        [jnp.stack([cosine, sine_part], 1), jnp.stack([-sine_part, cosine], 1)], 0
    ).astype(jnp.bfloat16)


def depth_tables(grid_z, steps, modes_z, modes_t):
    along_z = phase_angles(modes_z, jnp.arange(grid_z, dtype=jnp.int32), grid_z)
    time_freq = jnp.arange(modes_t, dtype=jnp.int32)
    time_pos = jnp.arange(steps, dtype=jnp.int32)
    along_t = (
        2.0
        * math.pi
        * jnp.mod(time_freq[:, None] * time_pos[None, :], steps).astype(jnp.float32)
        / steps
    )
    angles = along_z[:, None, :, None] + along_t[None, :, None, :]
    cosine = jnp.cos(angles)
    sine_part = jnp.sin(angles)
    forward = jnp.stack([cosine, -sine_part], 2) / math.sqrt(grid_z * steps)
    forward = forward.reshape(2 * modes_z * modes_t, grid_z * steps).T.astype(jnp.bfloat16)
    factor = jnp.where(time_freq == 0, 1.0, 2.0).astype(jnp.float32)[
        None, :, None, None
    ] / math.sqrt(modes_z * modes_t)
    inverse = jnp.stack([factor * cosine, -factor * sine_part], 2)
    inverse = inverse.reshape(2 * modes_z * modes_t, grid_z * steps).astype(jnp.bfloat16)
    return (forward, inverse)


def local(features, mode_weights, point_weight, bias_term, conv_weight):
    flt = jnp.float32
    local_x, local_y, channels, depth = features.shape
    grid_x = local_x * lax.axis_size("gx")
    grid_y = local_y * lax.axis_size("gy")
    modes_local = mode_weights.shape[0]
    modes_ky = mode_weights.shape[1]
    modes_kx = mode_weights.shape[5]
    rows_mine = modes_local * modes_ky // lax.axis_size("gx")
    zt_forward, zt_inverse = depth_tables(GRID_Z, STEPS, MZ, MT)
    first_section = jnp.einsum(
        "xycs,sq->qxcy", features, zt_forward, preferred_element_type=flt
    ).astype(jnp.bfloat16)
    y_forward = forward_table(modes_ky, jnp.arange(grid_y, dtype=jnp.int32), grid_y)
    blocks = lax.all_to_all(first_section, "gy", split_axis=0, concat_axis=3, tiled=True)
    shaped = blocks.reshape(modes_local, 2, blocks.shape[1], channels, grid_y)
    second = jnp.einsum("mrxcy,rysk->mkscx", shaped, y_forward, preferred_element_type=flt).astype(
        jnp.bfloat16
    )
    second = second.reshape(modes_local * modes_ky, 2, channels, local_x)
    place_x = lax.axis_index("gx")
    x_forward = forward_table(modes_kx, jnp.arange(grid_x, dtype=jnp.int32), grid_x)
    third = jnp.einsum(
        "jrcx,rxsk->jsck",
        lax.all_to_all(second, "gx", split_axis=0, concat_axis=3, tiled=True),
        x_forward,
        preferred_element_type=flt,
    )
    weights_flat = mode_weights.reshape(modes_local * modes_ky, 2, channels, channels, modes_kx)
    chosen = lax.dynamic_slice_in_dim(weights_flat, place_x * rows_mine, rows_mine, 0).astype(flt)
    highest = lax.Precision.HIGHEST

    def contract(weight_part, value_part):
        return jnp.einsum("jcok,jck->jok", weight_part, value_part, precision=highest)

    real_part = contract(chosen[:, 0], third[:, 0]) - contract(chosen[:, 1], third[:, 1])
    imag_part = contract(chosen[:, 0], third[:, 1]) + contract(chosen[:, 1], third[:, 0])
    mixed_modes = jnp.stack([real_part, imag_part], 1).astype(jnp.bfloat16)
    x_back = inverse_table(modes_kx, jnp.arange(grid_x, dtype=jnp.int32), grid_x)
    back_x = jnp.einsum("jrck,rksx->jscx", mixed_modes, x_back, preferred_element_type=flt).astype(
        jnp.bfloat16
    )
    returned = lax.all_to_all(back_x, "gx", split_axis=3, concat_axis=0, tiled=True)
    shaped_back = returned.reshape(modes_local, modes_ky, 2, channels, local_x)
    y_back = inverse_table(modes_ky, jnp.arange(grid_y, dtype=jnp.int32), grid_y)
    back_y = jnp.einsum(
        "mkrcx,rksy->msxcy", shaped_back, y_back, preferred_element_type=flt
    ).astype(jnp.bfloat16)
    back_y = back_y.reshape(2 * modes_local, local_x, channels, grid_y)
    full_modes = lax.all_to_all(back_y, "gy", split_axis=3, concat_axis=0, tiled=True)
    spectral = jnp.einsum("qxcy,qs->xycs", full_modes, zt_inverse, preferred_element_type=flt)
    half_x = local_x // 2
    half_y = local_y // 2
    half_depth = depth // 2
    pooled = features.reshape(half_x, 2, half_y, 2, channels, GRID_Z // 2, 2, STEPS).astype(flt)
    pooled = (
        pooled.mean(axis=(1, 3, 6))
        .reshape(half_x, half_y, channels, half_depth)
        .astype(jnp.bfloat16)
    )
    rimmed = with_halo(pooled, (("gx", 0), ("gy", 1)), 1)
    padded = jnp.pad(rimmed, ((0, 0), (0, 0), (0, 0), (STEPS, STEPS)))
    summed = jnp.zeros((half_x, half_y, channels, half_depth), flt)
    for offset in range(27):
        move_x = offset // 9
        move_y = offset // 3 % 3
        move_z = offset % 3
        window = padded[
            move_x : move_x + half_x,
            move_y : move_y + half_y,
            :,
            move_z * STEPS : move_z * STEPS + half_depth,
        ]
        summed = summed + jnp.einsum(
            "xycs,co->xyos", window, conv_weight[offset], preferred_element_type=flt
        )
    coarse = jax.nn.gelu(summed).reshape(half_x, 1, half_y, 1, channels, GRID_Z // 2, 1, STEPS)
    upsampled = jnp.broadcast_to(coarse, (half_x, 2, half_y, 2, channels, GRID_Z // 2, 2, STEPS))
    upsampled = upsampled.reshape(local_x, local_y, channels, depth)
    pointwise = jnp.einsum("xycs,co->xyos", features, point_weight, preferred_element_type=flt)
    return jax.nn.gelu(spectral + upsampled + pointwise + bias_term[None, None, :, None]).astype(
        jnp.bfloat16
    )


def solution(mesh):
    in_specs = (P("gx", "gy", None, None), P("gy", None, None, None, None, None), P(), P(), P())
    out_specs = P("gx", "gy", None, None)
    return jax.shard_map(local, mesh=mesh, in_specs=in_specs, out_specs=out_specs, check_vma=False)
```

profile of v0, /device:TPU:1, one launch (start us, length us, event | category | flops | bytes accessed | tf_op | source)
XLA Modules:
  0.0 177.8 jit_solution(8296176580318824428)
XLA Ops:
  2.2 3.0 %reshape.410 = bf16[128,512,1,1]{1,0,2,3:T(8,128)(2,1)S(1)} reshape(bf16[16,4,2,64,8]{4,3,2,1,0:T(8,128)(2,1)S(1)} %copy.224) | data formatting | bytes 262144 | tf_op jit(solution)/shard_map/convert_element_type | solution.py:72
  6.6 2.6 %reshape.462 = bf16[32,2,1152]{2,1,0:T(2,128)(2,1)} reshape(bf16[128,8,4,18]{3,2,1,0:T(4,128)(2,1)S(1)} %bitcast.422) | data formatting | bytes 294912
  9.3 13.0 %all-to-all-start = ((bf16[32,2,1152]{2,1,0:T(2,128)(2,1)}), bf16[32,2,1152]{2,1,0:T(2,128)(2,1)S(1)}, u32[]{:S(2)}, u32[]{:S(2)}) async-start(bf16[32,2,1152]{2,1,0:T(2,128)(2,1)} %reshape.462), calls=%async_computation | async-start | bytes 294912 | tf_op jit(solution)/shard_map/all_to_all | solution.py:95
  22.2 4.3 %copy.245 = f32[8,4,18,512]{2,3,1,0:T(8,128)} copy(bf16[8,4,18,512]{3,1,2,0:T(4,128)(2,1)S(1)} %copy-done.3) | data formatting | bytes 1769472 | tf_op jit(solution)/shard_map/convert_element_type | solution.py:135
  26.5 4.4 %reduce_sum.9 = f32[4,2,18,32,8]{2,4,3,1,0:T(8,128)S(1)} reduce(f32[4,2,2,2,18,32,2,8]{4,7,6,5,3,2,1,0:T(8,128)} %bitcast.419, f32[]{:T(128)} %constant.120.clone.1), dimensions={1,3,6}, to_apply=%region_0.1 | reduce | flops 258048 | bytes 1327108 | tf_op jit(solution)/shard_map/reduce_sum | solution.py:137
  31.7 4.8 %collective-permute-start = (bf16[1,2,18,256]{3,2,1,0:T(8,128)(2,1)}, bf16[1,2,18,256]{3,2,1,0:T(8,128)(2,1)}, u32[]{:S(2)}, u32[]{:S(2)}) collective-permute-start(bf16[1,2,18,256]{3,2,1,0:T(8,128)(2,1)} %copy.246), channel_id=1, source_target_pairs={{0,32},{32,64},{64,96},{96,128},{128,160},{160,192},{192,224},{224... | collective-permute-start | bytes 55304 | tf_op jit(solution)/shard_map/ppermute | solution.py:19
  44.1 8.7 %copy.234 = bf16[2,24,2,18,18,24]{5,4,3,1,0,2:T(8,128)(2,1)} copy(bf16[2,24,2,18,18,24]{5,2,4,3,1,0:T(2,128)(2,1)} %param.6) | data formatting | bytes 2985984 | tf_op args[1]
  59.9 1.8 copy.367
  71.2 1.7 copy.374
  82.6 3.0 %reshape.431 = bf16[128,512,1,1]{1,0,2,3:T(8,128)(2,1)S(1)} reshape(bf16[16,4,2,64,8]{4,3,2,1,0:T(8,128)(2,1)S(1)} %copy.221) | data formatting | bytes 262144 | tf_op jit(solution)/shard_map/convert_element_type | solution.py:77
  86.4 3.8 %collective-permute-start.2 = (bf16[6,1,18,256]{3,2,1,0:T(8,128)(2,1)S(1)}, bf16[6,1,18,256]{3,2,1,0:T(8,128)(2,1)S(1)}, u32[]{:S(2)}, u32[]{:S(2)}) collective-permute-start(bf16[6,1,18,256]{3,2,1,0:T(8,128)(2,1)S(1)} %get-tuple-element.13), channel_id=1, source_target_pairs={{0,1},{1,2},{2,3},{3,4},{4,5},{5,6},{6,7},{7,8},{8,9},{9,10},{10,1... | collective-permute-start | bytes 165896 | tf_op jit(solution)/shard_map/ppermute | solution.py:19
  90.2 2.1 %collective-permute-start.3 = (bf16[6,1,18,256]{3,2,1,0:T(8,128)(2,1)S(1)}, bf16[6,1,18,256]{3,2,1,0:T(8,128)(2,1)S(1)}, u32[]{:S(2)}, u32[]{:S(2)}) collective-permute-start(bf16[6,1,18,256]{3,2,1,0:T(8,128)(2,1)S(1)} %get-tuple-element.14), channel_id=1, source_target_pairs={{1,0},{2,1},{3,2},{4,3},{5,4},{6,5},{7,6},{8,7},{9,8},{10,9},{11,1... | collective-permute-start | bytes 165896 | tf_op jit(solution)/shard_map/ppermute | solution.py:22
  92.6 3.3 %collective-permute-done.3 = bf16[6,1,18,256]{3,2,1,0:T(8,128)(2,1)S(1)} collective-permute-done((bf16[6,1,18,256]{3,2,1,0:T(8,128)(2,1)S(1)}, bf16[6,1,18,256]{3,2,1,0:T(8,128)(2,1)S(1)}, u32[]{:S(2)}, u32[]{:S(2)}) %collective-permute-start.3) | collective-permute-done | bytes 55328 | tf_op jit(solution)/shard_map/ppermute | solution.py:22
  103.9 2.6 %reshape.463 = bf16[128,8,4,18]{3,2,1,0:T(4,128)(2,1)S(1)} reshape(bf16[32,2,1152]{2,1,0:T(2,128)(2,1)S(1)} %all-to-all-done) | data formatting | bytes 294912
  108.7 10.1 %all-to-all-start.1 = ((bf16[16,2,432]{2,1,0:T(2,128)(2,1)}), bf16[16,2,432]{2,1,0:T(2,128)(2,1)S(1)}, u32[]{:S(2)}, u32[]{:S(2)}) async-start(bf16[16,2,432]{2,1,0:T(2,128)(2,1)} %reshape.464), calls=%async_computation.1 | async-start | bytes 65536 | tf_op jit(solution)/shard_map/all_to_all | solution.py:105
  119.0 8.7 %all-to-all-done.1 = bf16[16,2,432]{2,1,0:T(2,128)(2,1)S(1)} async-done(((bf16[16,2,432]{2,1,0:T(2,128)(2,1)}), bf16[16,2,432]{2,1,0:T(2,128)(2,1)S(1)}, u32[]{:S(2)}, u32[]{:S(2)}) %all-to-all-start.1) | async-done | bytes 27680 | tf_op jit(solution)/shard_map/all_to_all | solution.py:105
  130.9 3.5 %all-to-all-start.2 = ((bf16[16,2,432]{2,1,0:T(2,128)(2,1)}), bf16[16,2,432]{2,1,0:T(2,128)(2,1)S(1)}, u32[]{:S(2)}, u32[]{:S(2)}) async-start(bf16[16,2,432]{2,1,0:T(2,128)(2,1)} %reshape.466), calls=%async_computation.2 | async-start | bytes 65536 | tf_op jit(solution)/shard_map/all_to_all | solution.py:123
  134.7 8.5 %all-to-all-done.2 = bf16[16,2,432]{2,1,0:T(2,128)(2,1)S(1)} async-done(((bf16[16,2,432]{2,1,0:T(2,128)(2,1)}), bf16[16,2,432]{2,1,0:T(2,128)(2,1)S(1)}, u32[]{:S(2)}, u32[]{:S(2)}) %all-to-all-start.2) | async-done | bytes 27680 | tf_op jit(solution)/shard_map/all_to_all | solution.py:123
  145.8 2.6 %reshape.468 = bf16[32,2,1152]{2,1,0:T(2,128)(2,1)} reshape(bf16[128,4,8,18]{3,2,1,0:T(8,128)(2,1)S(1)} %bitcast.423) | data formatting | bytes 294912
  148.4 10.4 %all-to-all-start.3 = ((bf16[32,2,1152]{2,1,0:T(2,128)(2,1)}), bf16[32,2,1152]{2,1,0:T(2,128)(2,1)S(1)}, u32[]{:S(2)}, u32[]{:S(2)}) async-start(bf16[32,2,1152]{2,1,0:T(2,128)(2,1)} %reshape.468), calls=%async_computation.3 | async-start | bytes 294912 | tf_op jit(solution)/shard_map/all_to_all | solution.py:130
  159.6 4.0 %broadcast_in_dim.15 = f32[4,2,2,2,18,32,2,8]{4,7,6,5,3,2,1,0:T(8,128)} broadcast(f32[4,2,18,32,8]{2,4,3,1,0:T(8,128)S(1)} %bitcast.421), dimensions={0,2,4,5,7} | broadcast | bytes 1327104 | tf_op jit(solution)/shard_map/broadcast_in_dim | solution.py:158
  163.6 6.2 %copy.280 = f32[8,4,18,512]{3,0,2,1:T(8,128)} copy(f32[8,4,18,512]{2,3,1,0:T(8,128)} %bitcast.418) | data formatting | bytes 2359296 | tf_op jit(solution)/shard_map/reshape | solution.py:159
  169.8 2.6 %reshape.469 = bf16[128,4,8,18]{3,2,1,0:T(8,128)(2,1)S(1)} reshape(bf16[32,2,1152]{2,1,0:T(2,128)(2,1)S(1)} %all-to-all-done.3) | data formatting | bytes 294912
  173.8 2.8 %fusion.10 = bf16[8,4,18,512]{3,0,2,1:T(8,128)(2,1)S(1)} fusion(f32[8,4,18,512]{3,0,2,1:T(8,128)} %copy.280, bf16[128,512,1,1]{1,0,2,3:T(8,128)(2,1)S(1)} %reshape.431, bf16[128,8,18,4]{0,1,2,3:T(8,128)(2,1)S(1)} %copy.323, f32[18,8,4,512]{3,0,2,1:T(8,128)} %fusion.37, f32[18]{0:T(128)S(1)} %copy-done.40), kind=kOutput, calls=%fused_computation.16 | convolution fusion | flops 79036416 | bytes 3227720 | tf_op jit(solution)/shard_map/qxcy,qs->xycs/dot_general | solution.py:131
  (196 shorter events, 58.3 us)
Async XLA Ops:
  0.0 41.2 %copy-start = (bf16[18,18]{1,0:T(8,128)(2,1)S(1)}, bf16[18,18]{1,0:T(8,128)(2,1)}, u32[]{:S(2)}) copy-start(bf16[18,18]{1,0:T(8,128)(2,1)} %param.7) | copy-start | bytes 1948
  9.3 94.7 %all-to-all-start = ((bf16[32,2,1152]{2,1,0:T(2,128)(2,1)}), bf16[32,2,1152]{2,1,0:T(2,128)(2,1)S(1)}, u32[]{:S(2)}, u32[]{:S(2)}) async-start(bf16[32,2,1152]{2,1,0:T(2,128)(2,1)} %reshape.462), calls=%async_computation | async-start | bytes 294912 | tf_op jit(solution)/shard_map/all_to_all | solution.py:95
  31.0 8.2 %copy-start.2 = (bf16[27,18,18]{0,2,1:T(8,128)(2,1)S(1)}, bf16[27,18,18]{0,2,1:T(8,128)(2,1)}, u32[]{:S(2)}) copy-start(bf16[27,18,18]{0,2,1:T(8,128)(2,1)} %param.9) | copy-start | bytes 52492
  31.7 53.8 %collective-permute-start = (bf16[1,2,18,256]{3,2,1,0:T(8,128)(2,1)}, bf16[1,2,18,256]{3,2,1,0:T(8,128)(2,1)}, u32[]{:S(2)}, u32[]{:S(2)}) collective-permute-start(bf16[1,2,18,256]{3,2,1,0:T(8,128)(2,1)} %copy.246), channel_id=1, source_target_pairs={{0,32},{32,64},{64,96},{96,128},{128,160},{160,192},{192,224},{224... | collective-permute-start | bytes 55304 | tf_op jit(solution)/shard_map/ppermute | solution.py:19
  37.3 48.3 %collective-permute-start.1 = (bf16[1,2,18,256]{3,2,1,0:T(8,128)(2,1)}, bf16[1,2,18,256]{3,2,1,0:T(8,128)(2,1)S(1)}, u32[]{:S(2)}, u32[]{:S(2)}) collective-permute-start(bf16[1,2,18,256]{3,2,1,0:T(8,128)(2,1)} %copy.247), channel_id=1, source_target_pairs={{32,0},{64,32},{96,64},{128,96},{160,128},{192,160},{224,192},{256... | collective-permute-start | bytes 55304 | tf_op jit(solution)/shard_map/ppermute | solution.py:22
  53.0 20.0 %copy-start.9 = (bf16[1,18,18]{0,2,1:T(8,128)(2,1)S(1)}, bf16[1,18,18]{0,2,1:T(8,128)(2,1)}, u32[]{:S(2)}) copy-start(bf16[1,18,18]{0,2,1:T(8,128)(2,1)} %get-tuple-element.23) | copy-start | bytes 1948
  53.0 20.9 %copy-start.8 = (bf16[1,18,18]{0,2,1:T(8,128)(2,1)S(1)}, bf16[1,18,18]{0,2,1:T(8,128)(2,1)}, u32[]{:S(2)}) copy-start(bf16[1,18,18]{0,2,1:T(8,128)(2,1)} %get-tuple-element.24) | copy-start | bytes 1948
  53.0 21.7 %copy-start.7 = (bf16[1,18,18]{0,2,1:T(8,128)(2,1)S(1)}, bf16[1,18,18]{0,2,1:T(8,128)(2,1)}, u32[]{:S(2)}) copy-start(bf16[1,18,18]{0,2,1:T(8,128)(2,1)} %get-tuple-element.25) | copy-start | bytes 1948
  53.0 22.6 %copy-start.6 = (bf16[1,18,18]{0,2,1:T(8,128)(2,1)S(1)}, bf16[1,18,18]{0,2,1:T(8,128)(2,1)}, u32[]{:S(2)}) copy-start(bf16[1,18,18]{0,2,1:T(8,128)(2,1)} %get-tuple-element.20) | copy-start | bytes 1948
  53.0 23.4 %copy-start.5 = (bf16[1,18,18]{0,2,1:T(8,128)(2,1)S(1)}, bf16[1,18,18]{0,2,1:T(8,128)(2,1)}, u32[]{:S(2)}) copy-start(bf16[1,18,18]{0,2,1:T(8,128)(2,1)} %get-tuple-element.21) | copy-start | bytes 1948
  85.5 11.4 %copy-start.27 = (bf16[1,18,18]{1,2,0:T(8,128)(2,1)S(1)}, bf16[1,18,18]{1,2,0:T(8,128)(2,1)}, u32[]{:S(2)}) copy-start(bf16[1,18,18]{1,2,0:T(8,128)(2,1)} %copy.368) | copy-start | bytes 1948
  85.5 11.6 %copy-start.28 = (bf16[1,18,18]{1,2,0:T(8,128)(2,1)S(1)}, bf16[1,18,18]{1,2,0:T(8,128)(2,1)}, u32[]{:S(2)}) copy-start(bf16[1,18,18]{1,2,0:T(8,128)(2,1)} %copy.366) | copy-start | bytes 1948
  85.5 11.8 %copy-start.29 = (bf16[1,18,18]{1,2,0:T(8,128)(2,1)S(1)}, bf16[1,18,18]{1,2,0:T(8,128)(2,1)}, u32[]{:S(2)}) copy-start(bf16[1,18,18]{1,2,0:T(8,128)(2,1)} %copy.365) | copy-start | bytes 1948
  85.6 7.0 %copy-start.10 = (bf16[1,2,18,256]{3,2,1,0:T(8,128)(2,1)}, bf16[1,2,18,256]{3,2,1,0:T(8,128)(2,1)S(1)}, u32[]{:S(2)}) copy-start(bf16[1,2,18,256]{3,2,1,0:T(8,128)(2,1)S(1)} %collective-permute-done.1) | copy-start | bytes 55300
  86.3 11.2 %copy-start.30 = (bf16[1,18,18]{1,2,0:T(8,128)(2,1)S(1)}, bf16[1,18,18]{1,2,0:T(8,128)(2,1)}, u32[]{:S(2)}) copy-start(bf16[1,18,18]{1,2,0:T(8,128)(2,1)} %copy.371) | copy-start | bytes 1948
  86.4 11.4 %copy-start.31 = (bf16[1,18,18]{1,2,0:T(8,128)(2,1)S(1)}, bf16[1,18,18]{1,2,0:T(8,128)(2,1)}, u32[]{:S(2)}) copy-start(bf16[1,18,18]{1,2,0:T(8,128)(2,1)} %copy.377) | copy-start | bytes 1948
  86.4 6.2 %collective-permute-start.2 = (bf16[6,1,18,256]{3,2,1,0:T(8,128)(2,1)S(1)}, bf16[6,1,18,256]{3,2,1,0:T(8,128)(2,1)S(1)}, u32[]{:S(2)}, u32[]{:S(2)}) collective-permute-start(bf16[6,1,18,256]{3,2,1,0:T(8,128)(2,1)S(1)} %get-tuple-element.13), channel_id=1, source_target_pairs={{0,1},{1,2},{2,3},{3,4},{4,5},{5,6},{6,7},{7,8},{8,9},{9,10},{10,1... | collective-permute-start | bytes 165896 | tf_op jit(solution)/shard_map/ppermute | solution.py:19
  90.2 5.7 %collective-permute-start.3 = (bf16[6,1,18,256]{3,2,1,0:T(8,128)(2,1)S(1)}, bf16[6,1,18,256]{3,2,1,0:T(8,128)(2,1)S(1)}, u32[]{:S(2)}, u32[]{:S(2)}) collective-permute-start(bf16[6,1,18,256]{3,2,1,0:T(8,128)(2,1)S(1)} %get-tuple-element.14), channel_id=1, source_target_pairs={{1,0},{2,1},{3,2},{4,3},{5,4},{6,5},{7,6},{8,7},{9,8},{10,9},{11,1... | collective-permute-start | bytes 165896 | tf_op jit(solution)/shard_map/ppermute | solution.py:22
  108.7 18.9 %all-to-all-start.1 = ((bf16[16,2,432]{2,1,0:T(2,128)(2,1)}), bf16[16,2,432]{2,1,0:T(2,128)(2,1)S(1)}, u32[]{:S(2)}, u32[]{:S(2)}) async-start(bf16[16,2,432]{2,1,0:T(2,128)(2,1)} %reshape.464), calls=%async_computation.1 | async-start | bytes 65536 | tf_op jit(solution)/shard_map/all_to_all | solution.py:105
  118.8 10.9 %copy-start.14 = (bf16[1,24,2,128]{3,1,0,2:T(8,128)(2,1)S(1)}, bf16[1,24,2,128]{3,1,0,2:T(8,128)(2,1)}, u32[]{:S(2)}) copy-start(bf16[1,24,2,128]{3,1,0,2:T(8,128)(2,1)} %get-tuple-element.48) | copy-start | bytes 36868
  118.8 10.9 %copy-start.15 = (bf16[1,24,2,128]{3,1,0,2:T(8,128)(2,1)S(1)}, bf16[1,24,2,128]{3,1,0,2:T(8,128)(2,1)}, u32[]{:S(2)}) copy-start(bf16[1,24,2,128]{3,1,0,2:T(8,128)(2,1)} %get-tuple-element.49) | copy-start | bytes 36868
  130.9 12.3 %all-to-all-start.2 = ((bf16[16,2,432]{2,1,0:T(2,128)(2,1)}), bf16[16,2,432]{2,1,0:T(2,128)(2,1)S(1)}, u32[]{:S(2)}, u32[]{:S(2)}) async-start(bf16[16,2,432]{2,1,0:T(2,128)(2,1)} %reshape.466), calls=%async_computation.2 | async-start | bytes 65536 | tf_op jit(solution)/shard_map/all_to_all | solution.py:123
  144.1 14.7 %copy-start.34 = (bf16[1,18,18]{1,2,0:T(8,128)(2,1)S(1)}, bf16[1,18,18]{1,2,0:T(8,128)(2,1)}, u32[]{:S(2)}) copy-start(bf16[1,18,18]{1,2,0:T(8,128)(2,1)} %copy.385) | copy-start | bytes 1948
  148.4 21.4 %all-to-all-start.3 = ((bf16[32,2,1152]{2,1,0:T(2,128)(2,1)}), bf16[32,2,1152]{2,1,0:T(2,128)(2,1)S(1)}, u32[]{:S(2)}, u32[]{:S(2)}) async-start(bf16[32,2,1152]{2,1,0:T(2,128)(2,1)} %reshape.468), calls=%async_computation.3 | async-start | bytes 294912 | tf_op jit(solution)/shard_map/all_to_all | solution.py:130
  (25 other events, 52.3 us)
where the time goes:
time: 179 us; the launch traced here: 178 us
  local copies, waits for them, and re-layouts  83.5 us (47%)
  starting transfers between devices  49.2 us (27%)
  waiting for transfers between devices  20.6 us (12%)
  matrix products  13 us (7%)
  other arithmetic  10.5 us (6%)
    unnamed x121, local copies, waits for them, and re-layouts  50.3 us
    all_to_all x1, starting transfers between devices, local(): lax.all_to_all(first_section, 'gy', split_axis=0, concat_axis=3, tiled=True)  13 us
    all_to_all x1, starting transfers between devices, local(): lax.all_to_all(back_y, 'gy', split_axis=3, concat_axis=0, tiled=True)  10.4 us
    all_to_all x1, starting transfers between devices, local(): lax.all_to_all(second, 'gx', split_axis=0, concat_axis=3, tiled=True)  10.1 us
    all_to_all x1, waiting for transfers between devices, local(): lax.all_to_all(second, 'gx', split_axis=0, concat_axis=3, tiled=True)  8.67 us
    ppermute x2, starting transfers between devices, with_halo(): lax.ppermute(lax.slice_in_dim(block, block.shape[dim] - width, None, axis...  8.65 us
    all_to_all x1, waiting for transfers between devices, local(): lax.all_to_all(back_x, 'gx', split_axis=3, concat_axis=0, tiled=True)  8.55 us
    dot_general x27, matrix products, local(): jnp.einsum('xycs,co->xyos', window, conv_weight[offset], preferred_elemen...  7.25 us
  transfers between devices with their start and end apart: 8, of which 3 were waited for; matrix products, arithmetic and copies ran while one was open for 43% of the time, Pallas kernels for 0%

commit v1 on v0

v1 whole, which is shorter than its diff:
```python
import math

import jax
import jax.numpy as jnp
import ml_dtypes
import numpy as np
from jax import lax
from jax.experimental import pallas as pl
from jax.experimental.pallas import tpu as pltpu
from jax.sharding import PartitionSpec as P

BF = jnp.bfloat16
FLT = jnp.float32
MESH = pl.DeviceIdType.MESH

GRID_Z, STEPS, CH = 64, 8, 18
MX, MY, MZ, MT = 24, 24, 16, 4
GX, GY = 16, 32
LX, LY = 8, 4
ROWS = LX * CH * LY
PAIR = 2 * CH * LY
DEPTH = GRID_Z * STEPS
HALF = DEPTH // 2
MODES = MZ * MT
JS = 8
SLOT = 32


def frequencies(number):
    places = np.arange(number, dtype=np.int32)
    return np.where(places < number // 2, places, places - number)


def angles_of(number, length):
    places = np.arange(length, dtype=np.int32)
    fraction = np.mod(frequencies(number)[:, None] * places[None, :], length).astype(np.float32)
    return np.float32(2.0 * math.pi) * (fraction / np.float32(length))


def rounded(table):
    return np.asarray(table, np.float32).astype(ml_dtypes.bfloat16).astype(np.float32)


def forward_table(number, length):
    angles = angles_of(number, length).T
    cosine = np.cos(angles) / np.float32(math.sqrt(length))
    sine = np.sin(angles) / np.float32(math.sqrt(length))
    return rounded(np.stack([np.stack([cosine, -sine], 1), np.stack([sine, cosine], 1)], 0))


def inverse_table(number, length):
    angles = angles_of(number, length)
    cosine = np.cos(angles) / np.float32(math.sqrt(number))
    sine = np.sin(angles) / np.float32(math.sqrt(number))
    return rounded(np.stack([np.stack([cosine, sine], 1), np.stack([-sine, cosine], 1)], 0))


def depth_tables():
    along_z = angles_of(MZ, GRID_Z)
    time_freq = np.arange(MT, dtype=np.int32)
    time_pos = np.arange(STEPS, dtype=np.int32)
    along_t = np.mod(time_freq[:, None] * time_pos[None, :], STEPS).astype(np.float32)
    along_t = np.float32(2.0 * math.pi) * along_t / np.float32(STEPS)
    angles = along_z[:, None, :, None] + along_t[None, :, None, :]
    cosine, sine = np.cos(angles), np.sin(angles)
    forward = np.stack([cosine, -sine], 2) / np.float32(math.sqrt(DEPTH))
    forward = forward.reshape(2 * MODES, DEPTH)
    factor = np.where(time_freq == 0, 1.0, 2.0).astype(np.float32)[None, :, None, None]
    factor = factor / np.float32(math.sqrt(MODES))
    inverse = np.stack([factor * cosine, -factor * sine], 2).reshape(2 * MODES, DEPTH)
    return rounded(forward), rounded(inverse)


def make_tables():
    zt_forward, zt_inverse = depth_tables()
    yf, yi = forward_table(MY, GY * LY), inverse_table(MY, GY * LY)
    xf, xi = forward_table(MX, GX * LX), inverse_table(MX, GX * LX)
    eye2 = np.eye(2, dtype=np.float32)
    per = MY // 8
    block = yf.reshape(2, GY, LY, 2, 8, per)
    ty = np.zeros((LY, 2, 8, JS, GY, 2, 2), np.float32)
    ty[:, :, :, : 2 * per] = np.einsum("rgysaj,mn->ymajsgnr", block, eye2).reshape(
        LY, 2, 8, 2 * per, GY, 2, 2
    )
    ty = ty.reshape(LY * GX * JS, GY * 4)
    eyex, eyec, eyey = np.eye(LX), np.eye(CH, SLOT), np.eye(LY)
    gather = np.einsum("xX,cC,y->xcyXC", eyex, eyec, np.ones(LY)).reshape(ROWS, LX * SLOT)
    block = xf.reshape(2, GX, 2, 4, 2, MX)
    eyej = np.eye(per)
    tx = np.zeros((GX, 2, JS, per, 2, 4, SLOT), np.float32)
    tx[:, :, : 2 * per, :, :, :, :MX] = np.einsum("rahusk,ij->ahirjsuk", block, eyej).reshape(
        GX, 2, 2 * per, per, 2, 4, MX
    )
    tx = tx.reshape(GX * 2 * JS, per * 2 * 4 * SLOT)
    block = xi.reshape(2, MX, 2, GX, 2, 4)
    tix = np.zeros((GX, 2, JS, per, 2, 4, SLOT), np.float32)
    tix[:, :, : 2 * per, :, :, :, :MX] = np.einsum("rksahu,ij->ahisjruk", block, eyej).reshape(
        GX, 2, 2 * per, per, 2, 4, MX
    )
    tix = tix.reshape(GX * 2 * JS, per * 2 * 4 * SLOT)
    block = yi.reshape(2, 8, per, 2, GY, LY)
    tiy = np.zeros((LY, GY, 2, 2, 2, 8, JS), np.float32)
    tiy[..., : 2 * per] = np.einsum("rajsgy,mn->ygmsnajr", block, eye2).reshape(
        LY, GY, 2, 2, 2, 8, 2 * per
    )
    tiy = tiy.reshape(LY * GY * 4, GX * JS)
    pair_pool = np.einsum("x,cC,yY->YCxcy", np.ones(2), np.eye(CH), np.repeat(np.eye(2), 2, 0))
    pair_pool = pair_pool.reshape(2 * CH, PAIR)
    lane_up = np.einsum("zZ,tT->ZTzt", np.repeat(np.eye(GRID_Z // 2), 2, 0), np.eye(STEPS))
    lane_up = lane_up.reshape(HALF, DEPTH)
    lane_pool = 0.125 * lane_up.T
    row_up = np.zeros((PAIR, 40), np.float32)
    row_up[:, : 2 * CH] = pair_pool.T
    spread_o = np.einsum("x,oO,y->xoyO", np.ones(2), np.eye(CH), np.ones(LY)).reshape(PAIR, CH)
    same = np.einsum("xX,oc,yY->xoyXcY", np.eye(2), np.ones((CH, CH)), eyey).reshape(PAIR, PAIR)
    conv_rows = np.zeros((2, 3, 40, 3, CH), np.float32)
    conv_lanes = np.zeros((2, 3, 3, CH, 3, 4, CH), np.float32)
    for at in range(2):
        for dz in range(3):
            conv_rows[at, dz, at * CH : (at + 1) * CH, dz] = np.eye(CH)
        for dx in range(3):
            for dy in range(3):
                conv_lanes[at, dx, dy, :, dx, dy + at] = np.eye(CH)
    conv_rows = conv_rows.reshape(2, 120, 3 * CH)
    conv_lanes = conv_lanes.reshape(2, 9 * CH, 12 * CH)
    return [
        np.asarray(t, np.float32).astype(ml_dtypes.bfloat16)
        for t in (
            zt_forward,
            ty,
            gather,
            tx,
            tix,
            gather.T,
            tiy,
            zt_inverse,
            pair_pool,
            lane_pool,
            lane_up,
            row_up,
            spread_o,
            same,
            conv_rows,
            conv_lanes,
        )
    ]


def mm(a, b):
    return jnp.dot(a, b, preferred_element_type=FLT)


def mm_nt(a, b):
    return lax.dot_general(a, b, (((1,), (1,)), ((), ())), preferred_element_type=FLT)


def mm_tn(a, b):
    return lax.dot_general(a, b, (((0,), (0,)), ((), ())), preferred_element_type=FLT)


def halves(value):
    high = value.astype(BF)
    return high, (value - high.astype(FLT)).astype(BF)


def kernel(*refs):
    (f_hbm, w_hbm, pw_hbm, bias_hbm, cw_hbm), refs = refs[:5], refs[5:]
    tables_hbm, refs = refs[:16], refs[16:]
    out_hbm, refs = refs[0], refs[1:]
    (f_in, w_in, pw_in, bias_in, cw_in), refs = refs[:5], refs[5:]
    tables, refs = refs[:16], refs[16:]
    (
        f_rows,
        send_one,
        recv_one,
        send_two,
        recv_two,
        send_three,
        recv_three,
        send_four,
        recv_four,
        pool,
        point,
        conv,
        w_wide,
        third,
        mixed,
        base,
        out_rows,
        in_sem,
        table_sem,
        send_sem,
        recv_sem,
        own_sem,
        halo_send,
        halo_recv,
        out_sem,
    ) = refs
    (
        t_zf,
        t_y,
        t_gather,
        t_x,
        t_ix,
        t_spread,
        t_iy,
        t_zi,
        t_pair_pool,
        t_lane_pool,
        t_lane_up,
        t_row_up,
        t_spread_o,
        t_same,
        t_conv_rows,
        t_conv_lanes,
    ) = tables
    gx = lax.axis_index("gx")
    gy = lax.axis_index("gy")
    barrier = pltpu.get_barrier_semaphore()

    def on_gx(step):
        return (lax.rem(gx + step, GX), gy)

    def on_gy(step):
        return (gx, lax.rem(gy + step, GY))

    def greet(target):
        pl.semaphore_signal(barrier, inc=1, device_id=target, device_id_type=MESH)

    mine = [
        pltpu.make_async_copy(f_hbm, f_in, in_sem.at[0]),
        pltpu.make_async_copy(
            w_hbm.at[gx // 8, pl.ds(3 * lax.rem(gx, 8), 3)], w_in, in_sem.at[1]
        ),
        pltpu.make_async_copy(pw_hbm, pw_in, in_sem.at[2]),
        pltpu.make_async_copy(bias_hbm, bias_in, in_sem.at[3]),
        pltpu.make_async_copy(cw_hbm, cw_in, in_sem.at[4]),
    ]
    loads = [
        pltpu.make_async_copy(tables_hbm[i], tables[i], table_sem.at[i]) for i in range(16)
    ]
    loads[0].start()
    mine[0].start()

    def greet_gy(step, _):
        greet(on_gy(step))
        return 0

    def greet_gx(step, _):
        greet(on_gx(step))
        return 0

    lax.fori_loop(1, GY, greet_gy, 0)
    lax.fori_loop(1, GX, greet_gx, 0)
    sides = [(dx, dy) for dx in (-1, 0, 1) for dy in (-1, 0, 1) if (dx, dy) != (0, 0)]

    def beside(dx, dy):
        return (lax.rem(gx + dx + GX, GX), lax.rem(gy + dy + GY, GY))

    for dx, dy in sides:
        if dx != 0 and dy != 0:
            greet(beside(dx, dy))
    for load in loads[1:]:
        load.start()
    for load in mine[1:]:
        load.start()

    mine[0].wait()
    loads[0].wait()
    f_rows[...] = f_in.reshape(ROWS, DEPTH)[...]
    hat = mm_nt(t_zf[...], f_rows[...]).astype(BF)
    send_one[...] = hat.reshape(GY, 4, ROWS)

    def all_to_all(at, count, source, target, me, place):
        own = pltpu.make_async_copy(source.at[me], target.at[me], own_sem.at[at])
        own.start()

        def send(step, _):
            to = place(step)
            pltpu.make_async_remote_copy(
                src_ref=source.at[to[1] if count == GY else to[0]],
                dst_ref=target.at[me],
                send_sem=send_sem.at[at],
                recv_sem=recv_sem.at[at],
                device_id=to,
                device_id_type=MESH,
            ).start()
            return 0

        lax.fori_loop(1, count, send, 0)

        def arrive():
            own.wait()
            part = target.at[pl.ds(0, count - 1)]
            pltpu.make_async_copy(part, part, recv_sem.at[at]).wait()

        def leave():
            part = source.at[pl.ds(0, count - 1)]
            pltpu.make_async_copy(part, part, send_sem.at[at]).wait()

        return arrive, leave

    pl.semaphore_wait(barrier, (GY - 1) + (GX - 1) + 4)
    arrive_one, leave_one = all_to_all(0, GY, send_one, recv_one, gy, on_gy)

    for i in (8, 9):
        loads[i].wait()
    for pair in range(LX // 2):
        rows = mm(t_pair_pool[...], f_rows[pair * PAIR : (pair + 1) * PAIR])
        high, low = halves(rows)
        cells = mm(high, t_lane_pool[...]) + mm(low, t_lane_pool[...])
        pool[pair + 1, 1:3] = cells.astype(BF).reshape(2, 9, 2, HALF)

    def rim(which, dx, dy):
        sx = {-1: pl.ds(1, 1), 0: pl.ds(1, 4), 1: pl.ds(4, 1)}[dx]
        tx = {-1: pl.ds(5, 1), 0: pl.ds(1, 4), 1: pl.ds(0, 1)}[dx]
        sy = {-1: pl.ds(1, 1), 0: pl.ds(1, 2), 1: pl.ds(2, 1)}[dy]
        ty = {-1: pl.ds(3, 1), 0: pl.ds(1, 2), 1: pl.ds(0, 1)}[dy]
        return pltpu.make_async_remote_copy(
            src_ref=pool.at[sx, sy],
            dst_ref=pool.at[tx, ty],
            send_sem=halo_send.at[which],
            recv_sem=halo_recv.at[which],
            device_id=beside(dx, dy),
            device_id_type=MESH,
        )

    rims = [rim(i, dx, dy) for i, (dx, dy) in enumerate(sides)]
    for copy in rims:
        copy.start()

    for i in range(1, 5):
        mine[i].wait()
    for i in range(11, 16):
        loads[i].wait()
    wide = mm_nt(t_spread_o[...], pw_in[...]).astype(BF)
    wide = mm_nt(wide, t_spread_o[...]).astype(BF)
    point[...] = wide * t_same[...]
    conv_sum = jnp.zeros((120, 12 * CH), FLT)
    for at in range(2):
        lanes = mm(cw_in[...], t_conv_lanes[at]).astype(BF)
        conv_sum = conv_sum + mm(t_conv_rows[at], lanes)
    conv[...] = conv_sum.astype(BF)

    def widen(at, _):
        w_wide[at, :, 0:MX] = w_in.reshape(3 * CH, CH, 2, MX)[at].astype(FLT).reshape(2 * CH, MX)
        return 0

    lax.fori_loop(0, 3 * CH, widen, 0)
    mixed[...] = jnp.zeros_like(mixed)

    for i in (1, 2):
        loads[i].wait()
    arrive_one()
    lane = lax.broadcasted_iota(jnp.int32, (GX * JS, ROWS), 1)
    part = mm(t_y[...], recv_one[...].reshape(4 * GY, ROWS)).reshape(LY, GX * JS, ROWS)
    chosen = part[0]
    for y in range(1, LY):
        chosen = jnp.where(lax.rem(lane, LY) == y, part[y], chosen)
    high, low = halves(chosen)
    second = mm(high, t_gather[...]) + mm(low, t_gather[...])
    second = [second[:, h * 128 : (h + 1) * 128].reshape(GX, JS, 128) for h in range(2)]
    send_two[...] = jnp.concatenate(second, axis=1).astype(BF)
    arrive_two, leave_two = all_to_all(1, GX, send_two, recv_two, gx, on_gx)

    for i in (10,):
        loads[i].wait()
    for copy in rims:
        copy.wait_recv()

    @pl.when(gx == 0)
    def _():
        pool[0] = jnp.zeros((4, 9, 2, HALF), BF)

    @pl.when(gx == GX - 1)
    def _():
        pool[5] = jnp.zeros((4, 9, 2, HALF), BF)

    @pl.when(gy == 0)
    def _():
        pool[:, 0] = jnp.zeros((6, 9, 2, HALF), BF)

    @pl.when(gy == GY - 1)
    def _():
        pool[:, 3] = jnp.zeros((6, 9, 2, HALF), BF)

    column = jnp.sum(t_spread_o[...].astype(FLT) * bias_in[...], axis=1, keepdims=True)
    spot = lax.broadcasted_iota(jnp.int32, (40, HALF), 1)
    for pair in range(LX // 2):
        sums = mm(conv[...], pool[pair : pair + 3].reshape(12 * CH, HALF))
        below = jnp.where(spot >= STEPS, pltpu.roll(sums[0:40], STEPS, 1), 0.0)
        above = jnp.where(spot < HALF - STEPS, pltpu.roll(sums[80:120], HALF - STEPS, 1), 0.0)
        high, low = halves(jax.nn.gelu(sums[40:80] + below + above))
        span = slice(pair * PAIR, (pair + 1) * PAIR)
        up = mm(t_row_up[...], mm(high, t_lane_up[...]).astype(BF))
        up = up + mm(t_row_up[...], mm(low, t_lane_up[...]).astype(BF))
        base[span] = mm(point[...], f_rows[span]) + up + column

    for i in (3, 4):
        loads[i].wait()
    arrive_two()
    turned = mm_tn(recv_two[...].reshape(GX * 2 * JS, 128), t_x[...])
    group = lax.broadcasted_iota(jnp.int32, (SLOT, 128), 1) // SLOT
    for at in range(6):
        acc = jnp.zeros((SLOT, 128), FLT)
        for u in range(4):
            piece = turned[u * SLOT : (u + 1) * SLOT, at * 128 : (at + 1) * 128]
            acc = acc + jnp.where(group == u, piece, 0.0)
        acc = acc + pltpu.roll(acc, 64, 1)
        acc = acc + pltpu.roll(acc, 32, 1)
        third[at] = acc

    for j in range(3):
        real = jnp.zeros((CH, 128), FLT)
        imag = jnp.zeros((CH, 128), FLT)
        for c in range(CH):
            w_real = w_wide[j * CH + c, pl.ds(0, CH, stride=2), :]
            w_imag = w_wide[j * CH + c, pl.ds(1, CH, stride=2), :]
            u_real = third[2 * j, c : c + 1, :]
            u_imag = third[2 * j + 1, c : c + 1, :]
            real = real + (w_real * u_real - w_imag * u_imag)
            imag = imag + (w_real * u_imag + w_imag * u_real)
        mixed[2 * j, 0:CH, 0:MX] = real[:, 0:MX]
        mixed[2 * j + 1, 0:CH, 0:MX] = imag[:, 0:MX]

    blocks = []
    for at in range(6):
        value = mixed[at]
        value = value + pltpu.roll(value, 32, 1)
        value = value + pltpu.roll(value, 64, 1)
        tall = [jnp.where(group == u, value, 0.0) for u in range(4)]
        blocks.append(jnp.concatenate(tall, axis=0).astype(BF))
    back = mm_nt(t_ix[...], jnp.concatenate(blocks, axis=1))
    send_three[...] = back.astype(BF).reshape(GX, 2 * JS, 128)
    arrive_three, leave_three = all_to_all(2, GX, send_three, recv_three, gx, on_gx)

    for i in (5, 6, 7):
        loads[i].wait()
    arrive_three()
    wide_in = recv_three[...].astype(FLT)
    sides_in = [wide_in[:, h * JS : (h + 1) * JS].reshape(GX * JS, 128) for h in range(2)]
    spread = mm(jnp.concatenate(sides_in, axis=1).astype(BF), t_spread[...]).astype(BF)
    part = mm(t_iy[...], spread).reshape(LY, 4 * GY, ROWS)
    chosen = part[0]
    for y in range(1, LY):
        chosen = jnp.where(lax.rem(lane, LY) == y, part[y], chosen)
    send_four[...] = chosen.astype(BF).reshape(GY, 4, ROWS)
    arrive_four, leave_four = all_to_all(3, GY, send_four, recv_four, gy, on_gy)

    arrive_four()
    columns = recv_four[...].reshape(4 * GY, ROWS).astype(FLT).T.astype(BF)
    stores = []
    for pair in range(LX // 2):
        span = slice(pair * PAIR, (pair + 1) * PAIR)
        total = mm(columns[span], t_zi[...]) + base[span]
        out_rows[pair * 36 : (pair + 1) * 36] = jax.nn.gelu(total).astype(BF).reshape(36, 4, DEPTH)
        store = pltpu.make_async_copy(
            out_rows.at[pl.ds(pair * 36, 36)],
            out_hbm.at[pl.ds(pair * 36, 36)],
            out_sem.at[pair],
        )
        store.start()
        stores.append(store)
    for leave in (leave_one, leave_two, leave_three, leave_four):
        leave()
    for copy in rims:
        copy.wait_send()
    for store in stores:
        store.wait()


def local(features, mode_weights, point_weight, bias_term, conv_weight):
    tables = make_tables()
    f = features.transpose(0, 2, 1, 3).reshape(LX * CH, LY, DEPTH)
    w = mode_weights.transpose(0, 1, 3, 4, 2, 5)
    taps = conv_weight.reshape(3, 3, 3, CH, CH).transpose(2, 4, 0, 1, 3).reshape(3 * CH, 9 * CH)
    operands = [f, w, point_weight, bias_term.reshape(1, CH), taps]
    vmem = [
        pltpu.VMEM(f.shape, BF),
        pltpu.VMEM((3,) + w.shape[2:], BF),
        pltpu.VMEM(point_weight.shape, BF),
        pltpu.VMEM((1, CH), FLT),
        pltpu.VMEM(taps.shape, BF),
    ]
    vmem += [pltpu.VMEM(t.shape, BF) for t in tables]
    vmem += [
        pltpu.VMEM((ROWS, DEPTH), BF),
        pltpu.VMEM((GY, 4, ROWS), BF),
        pltpu.VMEM((GY, 4, ROWS), BF),
        pltpu.VMEM((GX, 2 * JS, 128), BF),
        pltpu.VMEM((GX, 2 * JS, 128), BF),
        pltpu.VMEM((GX, 2 * JS, 128), BF),
        pltpu.VMEM((GX, 2 * JS, 128), BF),
        pltpu.VMEM((GY, 4, ROWS), BF),
        pltpu.VMEM((GY, 4, ROWS), BF),
        pltpu.VMEM((6, 4, 9, 2, HALF), BF),
        pltpu.VMEM((PAIR, PAIR), BF),
        pltpu.VMEM((120, 12 * CH), BF),
        pltpu.VMEM((3 * CH, 2 * CH, 128), FLT),
        pltpu.VMEM((6, SLOT, 128), FLT),
        pltpu.VMEM((6, SLOT, 128), FLT),
        pltpu.VMEM((ROWS, DEPTH), FLT),
        pltpu.VMEM(f.shape, BF),
        pltpu.SemaphoreType.DMA((5,)),
        pltpu.SemaphoreType.DMA((16,)),
        pltpu.SemaphoreType.DMA((4,)),
        pltpu.SemaphoreType.DMA((4,)),
        pltpu.SemaphoreType.DMA((4,)),
        pltpu.SemaphoreType.DMA((8,)),
        pltpu.SemaphoreType.DMA((8,)),
        pltpu.SemaphoreType.DMA((4,)),
    ]
    out = pl.pallas_call(
        kernel,
        out_shape=jax.ShapeDtypeStruct(f.shape, BF),
        in_specs=[pl.BlockSpec(memory_space=pl.ANY)] * (5 + len(tables)),
        out_specs=pl.BlockSpec(memory_space=pl.ANY),
        scratch_shapes=vmem,
        compiler_params=pltpu.CompilerParams(
            collective_id=0, has_side_effects=True, vmem_limit_bytes=48 << 20
        ),
        name="layer",
    )(*operands, *[jnp.asarray(t) for t in tables])
    return out.reshape(LX, CH, LY, DEPTH).transpose(0, 2, 1, 3)


def solution(mesh):
    in_specs = (P("gx", "gy", None, None), P("gy", None, None, None, None, None), P(), P(), P())
    out_specs = P("gx", "gy", None, None)
    return jax.shard_map(local, mesh=mesh, in_specs=in_specs, out_specs=out_specs, check_vma=False)
```

time: 179 us -> 66.5 us (0.37)
  local copies, waits for them, and re-layouts: 83.5 us -> 19.2 us
  starting transfers between devices: 49.2 us -> 0 us
  Pallas kernels: 0 us -> 46.5 us
  waiting for transfers between devices: 20.6 us -> 0 us
  matrix products: 13 us -> 0 us
  other arithmetic: 10.5 us -> 0 us
    pallas_call x0 -> x1, Pallas kernels: none -> 46.5 us  [local(): pl.pallas_call(kernel, out_shape=jax.ShapeDtypeStruct(f.shape, BF), in_sp...]
    all_to_all x4 -> x0, starting transfers between devices: 36.9 us -> none  [the longest x1 13 us: local(): lax.all_to_all(first_section, 'gy', split_axis=0, concat_axis=3, tiled=True)]
    unnamed x121 -> x40, local copies, waits for them, and re-layouts: 50.3 us -> 18.7 us
    all_to_all x4 -> x0, waiting for transfers between devices: 17.2 us -> none  [the longest x1 8.67 us: local(): lax.all_to_all(second, 'gx', split_axis=0, concat_axis=3, tiled=True)]
    convert_element_type x9 -> x0, local copies, waits for them, and re-layouts: 13.8 us -> none  [the longest x1 4.26 us: local(): features.reshape(half_x, 2, half_y, 2, channels, GRID_Z // 2, 2, STEPS)]
    dot_general x34 -> x0, matrix products: 13 us -> none  [the longest x27 7.25 us: local(): jnp.einsum('xycs,co->xyos', window, conv_weight[offset], preferred_elemen...]
    ppermute x4 -> x0, starting transfers between devices: 12.3 us -> none  [the longest x2 8.65 us: with_halo(): lax.ppermute(lax.slice_in_dim(block, block.shape[dim] - width, None, axis...]
    reshape x5 -> x1, local copies, waits for them, and re-layouts: 8.79 us -> 0.14 us  [local(): conv_weight.reshape(3, 3, 3, CH, CH).transpose(2, 4, 0, 1, 3)]
  transfers between devices with their start and end apart: 8 -> 0, of which waited for: 3 -> 0; matrix products, arithmetic and copies ran while one was open for 43% -> 0% of each run, Pallas kernels for 0% -> 0%
where the time goes in v1:
time: 66.5 us; the launch traced here: 65.7 us
  Pallas kernels  46.5 us (70%)
  local copies, waits for them, and re-layouts  19.2 us (29%)
    pallas_call x1, Pallas kernels, local(): pl.pallas_call(kernel, out_shape=jax.ShapeDtypeStruct(f.shape, BF), in_sp...  46.5 us
    unnamed x40, local copies, waits for them, and re-layouts  18.7 us

profile of v1, /device:TPU:1, one launch (start us, length us, event | category | flops | bytes accessed | tf_op | source)
XLA Modules:
  0.0 65.7 jit_solution(5886895703063736073)
XLA Ops:
  0.0 1.2 %copy.23 = bf16[27,18,18]{2,1,0:T(8,128)(2,1)S(1)} copy(bf16[27,18,18]{0,2,1:T(8,128)(2,1)} %param.25) | data formatting | bytes 34992 | tf_op args[4]
  1.2 0.3 copy.24
  1.5 0.1 reshape.18.refs_4_
  1.7 1.1 %copy-done = bf16[8,4,18,512]{3,1,2,0:T(4,128)(2,1)S(1)} copy-done((bf16[8,4,18,512]{3,1,2,0:T(4,128)(2,1)S(1)}, bf16[8,4,18,512]{3,1,2,0:T(4,128)(2,1)}, u32[]{:S(2)}) %copy-start) | copy-done | bytes 589848
  2.7 1.0 %copy-done.1 = bf16[256,768]{1,0:T(8,128)(2,1)S(1)} copy-done((bf16[256,768]{1,0:T(8,128)(2,1)S(1)}, bf16[256,768]{1,0:T(8,128)(2,1)}, u32[]{:S(2)}) %copy-start.1) | copy-done | bytes 393240
  3.7 1.0 %copy-done.2 = bf16[256,768]{1,0:T(8,128)(2,1)S(1)} copy-done((bf16[256,768]{1,0:T(8,128)(2,1)S(1)}, bf16[256,768]{1,0:T(8,128)(2,1)}, u32[]{:S(2)}) %copy-start.2) | copy-done | bytes 393240
  4.7 1.0 %copy-done.3 = bf16[256,576]{1,0:T(8,128)(2,1)S(1)} copy-done((bf16[256,576]{1,0:T(8,128)(2,1)S(1)}, bf16[256,576]{1,0:T(8,128)(2,1)}, u32[]{:S(2)}) %copy-start.3) | copy-done | bytes 294936
  5.7 1.0 %copy-done.4 = bf16[576,256]{1,0:T(8,128)(2,1)S(1)} copy-done((bf16[576,256]{1,0:T(8,128)(2,1)S(1)}, bf16[576,256]{1,0:T(8,128)(2,1)}, u32[]{:S(2)}) %copy-start.4) | copy-done | bytes 294936
  6.7 0.9 %copy-done.5 = bf16[256,512]{1,0:T(8,128)(2,1)S(1)} copy-done((bf16[256,512]{1,0:T(8,128)(2,1)S(1)}, bf16[256,512]{1,0:T(8,128)(2,1)}, u32[]{:S(2)}) %copy-start.5) | copy-done | bytes 262168
  7.6 0.9 %copy-done.6 = bf16[512,256]{1,0:T(8,128)(2,1)S(1)} copy-done((bf16[512,256]{1,0:T(8,128)(2,1)S(1)}, bf16[512,256]{1,0:T(8,128)(2,1)}, u32[]{:S(2)}) %copy-start.6) | copy-done | bytes 262168
  8.6 0.9 %copy-done.7 = bf16[2,162,216]{2,1,0:T(8,128)(2,1)S(1)} copy-done((bf16[2,162,216]{2,1,0:T(8,128)(2,1)S(1)}, bf16[2,162,216]{2,1,0:T(8,128)(2,1)}, u32[]{:S(2)}) %copy-start.7) | copy-done | bytes 139992
  9.5 0.9 %copy-done.8 = bf16[128,512]{1,0:T(8,128)(2,1)S(1)} copy-done((bf16[128,512]{1,0:T(8,128)(2,1)S(1)}, bf16[128,512]{1,0:T(8,128)(2,1)}, u32[]{:S(2)}) %copy-start.8) | copy-done | bytes 131096
  10.4 0.9 %copy-done.9 = bf16[512,128]{1,0:T(8,128)(2,1)S(1)} copy-done((bf16[512,128]{1,0:T(8,128)(2,1)S(1)}, bf16[512,128]{1,0:T(8,128)(2,1)}, u32[]{:S(2)}) %copy-start.9) | copy-done | bytes 131096
  11.3 0.9 %copy-done.10 = bf16[512,128]{1,0:T(8,128)(2,1)S(1)} copy-done((bf16[512,128]{1,0:T(8,128)(2,1)S(1)}, bf16[512,128]{1,0:T(8,128)(2,1)}, u32[]{:S(2)}) %copy-start.10) | copy-done | bytes 131096
  12.2 0.9 %copy-done.11 = bf16[128,512]{1,0:T(8,128)(2,1)S(1)} copy-done((bf16[128,512]{1,0:T(8,128)(2,1)S(1)}, bf16[128,512]{1,0:T(8,128)(2,1)}, u32[]{:S(2)}) %copy-start.11) | copy-done | bytes 131096
  13.1 0.9 %copy-done.12 = bf16[144,144]{1,0:T(8,128)(2,1)S(1)} copy-done((bf16[144,144]{1,0:T(8,128)(2,1)S(1)}, bf16[144,144]{1,0:T(8,128)(2,1)}, u32[]{:S(2)}) %copy-start.12) | copy-done | bytes 41496
  14.0 0.8 %copy-done.13 = bf16[2,120,54]{2,1,0:T(8,128)(2,1)S(1)} copy-done((bf16[2,120,54]{2,1,0:T(8,128)(2,1)S(1)}, bf16[2,120,54]{2,1,0:T(8,128)(2,1)}, u32[]{:S(2)}) %copy-start.13) | copy-done | bytes 25944
  14.8 0.8 %copy-done.14 = bf16[144,18]{1,0:T(8,128)(2,1)S(1)} copy-done((bf16[144,18]{1,0:T(8,128)(2,1)S(1)}, bf16[144,18]{1,0:T(8,128)(2,1)}, u32[]{:S(2)}) %copy-start.14) | copy-done | bytes 5208
  15.6 0.8 %copy-done.15 = bf16[144,40]{1,0:T(8,128)(2,1)S(1)} copy-done((bf16[144,40]{1,0:T(8,128)(2,1)S(1)}, bf16[144,40]{1,0:T(8,128)(2,1)}, u32[]{:S(2)}) %copy-start.15) | copy-done | bytes 11544
  16.3 0.7 %copy-done.16 = bf16[36,144]{1,0:T(8,128)(2,1)S(1)} copy-done((bf16[36,144]{1,0:T(8,128)(2,1)S(1)}, bf16[36,144]{1,0:T(8,128)(2,1)}, u32[]{:S(2)}) %copy-start.16) | copy-done | bytes 10392
  17.1 0.7 %copy-done.17 = bf16[18,18]{1,0:T(8,128)(2,1)S(1)} copy-done((bf16[18,18]{1,0:T(8,128)(2,1)S(1)}, bf16[18,18]{1,0:T(8,128)(2,1)}, u32[]{:S(2)}) %copy-start.17) | copy-done | bytes 672
  17.8 0.7 copy-done.18
  18.4 46.5 %layer.1 = bf16[144,4,512]{2,1,0:T(4,128)(2,1)S(1)} custom-call(bf16[144,4,512]{2,1,0:T(4,128)(2,1)S(1)} %bitcast.12, bf16[2,24,18,18,2,24]{5,4,3,2,1,0:T(2,128)(2,1)} %bitcast.14, bf16[18,18]{1,0:T(8,128)(2,1)S(1)} %copy-done.17, f32[1,18]{1,0:T(1,128)S(1)} %bitcast.13, bf16[54,162]{1,0:T(8,128)(2,1)S(1)} %reshape.18.refs_4_, ...), custom_call_target="tpu_custom_call" | custom-call | tf_op jit(solution)/shard_map/layer/pallas_call | solution.py:513
  64.9 0.8 %copy.26 = bf16[8,4,18,512]{3,1,2,0:T(4,128)(2,1)} copy(bf16[8,4,18,512]{3,1,2,0:T(4,128)(2,1)S(1)} %bitcast.11) | data formatting | bytes 1179648
  (19 shorter events, 0.0 us)
Async XLA Ops:
  1.7 1.1 %copy-start = (bf16[8,4,18,512]{3,1,2,0:T(4,128)(2,1)S(1)}, bf16[8,4,18,512]{3,1,2,0:T(4,128)(2,1)}, u32[]{:S(2)}) copy-start(bf16[8,4,18,512]{3,1,2,0:T(4,128)(2,1)} %param.21) | copy-start | bytes 1769476
  2.7 1.0 %copy-start.1 = (bf16[256,768]{1,0:T(8,128)(2,1)S(1)}, bf16[256,768]{1,0:T(8,128)(2,1)}, u32[]{:S(2)}) copy-start(bf16[256,768]{1,0:T(8,128)(2,1)} %constant.36.clone.refs_9_) | copy-start | bytes 1179652
  3.7 1.0 %copy-start.2 = (bf16[256,768]{1,0:T(8,128)(2,1)S(1)}, bf16[256,768]{1,0:T(8,128)(2,1)}, u32[]{:S(2)}) copy-start(bf16[256,768]{1,0:T(8,128)(2,1)} %constant.35.clone.refs_8_) | copy-start | bytes 1179652
  4.7 1.0 %copy-start.3 = (bf16[256,576]{1,0:T(8,128)(2,1)S(1)}, bf16[256,576]{1,0:T(8,128)(2,1)}, u32[]{:S(2)}) copy-start(bf16[256,576]{1,0:T(8,128)(2,1)} %constant.37.clone.refs_10_) | copy-start | bytes 884740
  5.7 1.0 %copy-start.4 = (bf16[576,256]{1,0:T(8,128)(2,1)S(1)}, bf16[576,256]{1,0:T(8,128)(2,1)}, u32[]{:S(2)}) copy-start(bf16[576,256]{1,0:T(8,128)(2,1)} %constant.34.clone.refs_7_) | copy-start | bytes 884740
  6.6 0.9 %copy-start.5 = (bf16[256,512]{1,0:T(8,128)(2,1)S(1)}, bf16[256,512]{1,0:T(8,128)(2,1)}, u32[]{:S(2)}) copy-start(bf16[256,512]{1,0:T(8,128)(2,1)} %constant.42.clone.refs_15_) | copy-start | bytes 786436
  7.6 0.9 %copy-start.6 = (bf16[512,256]{1,0:T(8,128)(2,1)S(1)}, bf16[512,256]{1,0:T(8,128)(2,1)}, u32[]{:S(2)}) copy-start(bf16[512,256]{1,0:T(8,128)(2,1)} %constant.41.clone.refs_14_) | copy-start | bytes 786436
  8.5 0.9 %copy-start.7 = (bf16[2,162,216]{2,1,0:T(8,128)(2,1)S(1)}, bf16[2,162,216]{2,1,0:T(8,128)(2,1)}, u32[]{:S(2)}) copy-start(bf16[2,162,216]{2,1,0:T(8,128)(2,1)} %constant.47.clone.refs_20_) | copy-start | bytes 419908
  9.5 0.9 %copy-start.8 = (bf16[128,512]{1,0:T(8,128)(2,1)S(1)}, bf16[128,512]{1,0:T(8,128)(2,1)}, u32[]{:S(2)}) copy-start(bf16[128,512]{1,0:T(8,128)(2,1)} %constant.39.clone.refs_12_) | copy-start | bytes 393220
  10.4 0.9 %copy-start.9 = (bf16[512,128]{1,0:T(8,128)(2,1)S(1)}, bf16[512,128]{1,0:T(8,128)(2,1)}, u32[]{:S(2)}) copy-start(bf16[512,128]{1,0:T(8,128)(2,1)} %constant.38.clone.refs_11_) | copy-start | bytes 393220
  11.3 0.9 %copy-start.10 = (bf16[512,128]{1,0:T(8,128)(2,1)S(1)}, bf16[512,128]{1,0:T(8,128)(2,1)}, u32[]{:S(2)}) copy-start(bf16[512,128]{1,0:T(8,128)(2,1)} %constant.33.clone.refs_6_) | copy-start | bytes 393220
  12.2 0.9 %copy-start.11 = (bf16[128,512]{1,0:T(8,128)(2,1)S(1)}, bf16[128,512]{1,0:T(8,128)(2,1)}, u32[]{:S(2)}) copy-start(bf16[128,512]{1,0:T(8,128)(2,1)} %constant.32.clone.refs_5_) | copy-start | bytes 393220
  13.1 0.9 %copy-start.12 = (bf16[144,144]{1,0:T(8,128)(2,1)S(1)}, bf16[144,144]{1,0:T(8,128)(2,1)}, u32[]{:S(2)}) copy-start(bf16[144,144]{1,0:T(8,128)(2,1)} %constant.45.clone.refs_18_) | copy-start | bytes 124420
  14.0 0.8 %copy-start.13 = (bf16[2,120,54]{2,1,0:T(8,128)(2,1)S(1)}, bf16[2,120,54]{2,1,0:T(8,128)(2,1)}, u32[]{:S(2)}) copy-start(bf16[2,120,54]{2,1,0:T(8,128)(2,1)} %constant.46.clone.refs_19_) | copy-start | bytes 77764
  14.8 0.8 %copy-start.14 = (bf16[144,18]{1,0:T(8,128)(2,1)S(1)}, bf16[144,18]{1,0:T(8,128)(2,1)}, u32[]{:S(2)}) copy-start(bf16[144,18]{1,0:T(8,128)(2,1)} %constant.44.clone.refs_17_) | copy-start | bytes 15556
  15.6 0.8 %copy-start.15 = (bf16[144,40]{1,0:T(8,128)(2,1)S(1)}, bf16[144,40]{1,0:T(8,128)(2,1)}, u32[]{:S(2)}) copy-start(bf16[144,40]{1,0:T(8,128)(2,1)} %constant.43.clone.refs_16_) | copy-start | bytes 34564
  16.3 0.7 %copy-start.16 = (bf16[36,144]{1,0:T(8,128)(2,1)S(1)}, bf16[36,144]{1,0:T(8,128)(2,1)}, u32[]{:S(2)}) copy-start(bf16[36,144]{1,0:T(8,128)(2,1)} %constant.40.clone.refs_13_) | copy-start | bytes 31108
  17.1 0.7 %copy-start.17 = (bf16[18,18]{1,0:T(8,128)(2,1)S(1)}, bf16[18,18]{1,0:T(8,128)(2,1)}, u32[]{:S(2)}) copy-start(bf16[18,18]{1,0:T(8,128)(2,1)} %refs_2_.1) | copy-start | bytes 1948
  17.8 0.7 copy-start.18

commit v2 on v1

--- a/solution.py
+++ b/solution.py
@@ -24,6 +24,7 @@
 MODES = MZ * MT
 JS = 8
 SLOT = 32
+TABLES = 17
 
 
 def frequencies(number):
@@ -109,20 +110,22 @@
     lane_up = np.einsum("zZ,tT->ZTzt", np.repeat(np.eye(GRID_Z // 2), 2, 0), np.eye(STEPS))
     lane_up = lane_up.reshape(HALF, DEPTH)
     lane_pool = 0.125 * lane_up.T
-    row_up = np.zeros((PAIR, 40), np.float32)
-    row_up[:, : 2 * CH] = pair_pool.T
+    row_up = np.zeros((PAIR, 2, 24), np.float32)
+    row_up[:, :, :CH] = pair_pool.T.reshape(PAIR, 2, CH)
+    row_up = row_up.reshape(PAIR, 48)
     spread_o = np.einsum("x,oO,y->xoyO", np.ones(2), np.eye(CH), np.ones(LY)).reshape(PAIR, CH)
     same = np.einsum("xX,oc,yY->xoyXcY", np.eye(2), np.ones((CH, CH)), eyey).reshape(PAIR, PAIR)
-    conv_rows = np.zeros((2, 3, 40, 3, CH), np.float32)
-    conv_lanes = np.zeros((2, 3, 3, CH, 3, 4, CH), np.float32)
-    for at in range(2):
-        for dz in range(3):
-            conv_rows[at, dz, at * CH : (at + 1) * CH, dz] = np.eye(CH)
-        for dx in range(3):
-            for dy in range(3):
-                conv_lanes[at, dx, dy, :, dx, dy + at] = np.eye(CH)
-    conv_rows = conv_rows.reshape(2, 120, 3 * CH)
-    conv_lanes = conv_lanes.reshape(2, 9 * CH, 12 * CH)
+    eyecc = np.eye(CH, dtype=np.float32)
+    conv_place = np.zeros((3, 2, 128, 3, 4, CH), np.float32)
+    for dx in range(3):
+        for dy in range(3):
+            for dz in range(3):
+                for at in range(2):
+                    conv_place[dz, at, 9 * dx + 3 * dy + dz, dx, dy + at] = 1.0
+    conv_place = conv_place.reshape(6, 128, 12 * CH)
+    conv_same = np.einsum("cC,o,d->coCd", eyecc, np.ones(24), np.ones(12))
+    conv_same = conv_same.transpose(0, 1, 3, 2).reshape(24 * CH, 12 * CH)
+    conv_sum = np.einsum("c,oO->ocO", np.ones(CH), np.eye(24)).reshape(24, 24 * CH)
     return [
         np.asarray(t, np.float32).astype(ml_dtypes.bfloat16)
         for t in (
@@ -140,8 +143,9 @@
             row_up,
             spread_o,
             same,
-            conv_rows,
-            conv_lanes,
+            conv_place,
+            conv_same,
+            conv_sum,
         )
     ]
 
@@ -165,10 +169,10 @@
 
 def kernel(*refs):
     (f_hbm, w_hbm, pw_hbm, bias_hbm, cw_hbm), refs = refs[:5], refs[5:]
-    tables_hbm, refs = refs[:16], refs[16:]
+    tables_hbm, refs = refs[:TABLES], refs[TABLES:]
     out_hbm, refs = refs[0], refs[1:]
     (f_in, w_in, pw_in, bias_in, cw_in), refs = refs[:5], refs[5:]
-    tables, refs = refs[:16], refs[16:]
+    tables, refs = refs[:TABLES], refs[TABLES:]
     (
         f_rows,
         send_one,
@@ -181,6 +185,7 @@
         recv_four,
         pool,
         point,
+        taps,
         conv,
         w_wide,
         third,
@@ -211,18 +216,27 @@
         t_row_up,
         t_spread_o,
         t_same,
-        t_conv_rows,
-        t_conv_lanes,
+        t_conv_place,
+        t_conv_same,
+        t_conv_sum,
     ) = tables
     gx = lax.axis_index("gx")
     gy = lax.axis_index("gy")
     barrier = pltpu.get_barrier_semaphore()
 
+    def far_first(step, count):
+        sign = 1 - 2 * lax.rem(step, 2)
+        return count // 2 + sign * lax.div(step + 1, 2)
+
     def on_gx(step):
-        return (lax.rem(gx + step, GX), gy)
+        x = lax.rem(lax.div(gx, 4) + far_first(lax.rem(step, 4), 4), 4)
+        y = lax.rem(lax.rem(gx, 4) + far_first(lax.div(step, 4), 4), 4)
+        return (4 * x + y, gy)
 
     def on_gy(step):
-        return (gx, lax.rem(gy + step, GY))
+        z = lax.rem(lax.div(gy, 4) + far_first(lax.div(step, 4), 8), 8)
+        low = lax.rem(lax.rem(gy, 4) + far_first(lax.rem(step, 4), 4), 4)
+        return (gx, 4 * z + low)
 
     def greet(target):
         pl.semaphore_signal(barrier, inc=1, device_id=target, device_id_type=MESH)
@@ -237,7 +251,7 @@
         pltpu.make_async_copy(cw_hbm, cw_in, in_sem.at[4]),
     ]
     loads = [
-        pltpu.make_async_copy(tables_hbm[i], tables[i], table_sem.at[i]) for i in range(16)
+        pltpu.make_async_copy(tables_hbm[i], tables[i], table_sem.at[i]) for i in range(TABLES)
     ]
     loads[0].start()
     mine[0].start()
@@ -250,8 +264,8 @@
         greet(on_gx(step))
         return 0
 
-    lax.fori_loop(1, GY, greet_gy, 0)
-    lax.fori_loop(1, GX, greet_gx, 0)
+    lax.fori_loop(0, GY - 1, greet_gy, 0)
+    lax.fori_loop(0, GX - 1, greet_gx, 0)
     sides = [(dx, dy) for dx in (-1, 0, 1) for dy in (-1, 0, 1) if (dx, dy) != (0, 0)]
 
     def beside(dx, dy):
@@ -287,7 +301,7 @@
             ).start()
             return 0
 
-        lax.fori_loop(1, count, send, 0)
+        lax.fori_loop(0, count - 1, send, 0)
 
         def arrive():
             own.wait()
@@ -331,16 +345,18 @@
 
     for i in range(1, 5):
         mine[i].wait()
-    for i in range(11, 16):
+    for i in range(11, TABLES):
         loads[i].wait()
     wide = mm_nt(t_spread_o[...], pw_in[...]).astype(BF)
     wide = mm_nt(wide, t_spread_o[...]).astype(BF)
     point[...] = wide * t_same[...]
-    conv_sum = jnp.zeros((120, 12 * CH), FLT)
-    for at in range(2):
-        lanes = mm(cw_in[...], t_conv_lanes[at]).astype(BF)
-        conv_sum = conv_sum + mm(t_conv_rows[at], lanes)
-    conv[...] = conv_sum.astype(BF)
+    taps[...] = jnp.zeros_like(taps)
+    for c in range(CH):
+        taps[c, 0:CH, 0:27] = cw_in[c].astype(FLT)
+    flat = taps[...].reshape(24 * CH, 128).astype(BF)
+    for at in range(6):
+        placed = mm(flat, t_conv_place[at]).astype(BF) * t_conv_same[...]
+        conv[at * 24 : (at + 1) * 24] = mm(t_conv_sum[...], placed)
 
     def widen(at, _):
         w_wide[at, :, 0:MX] = w_in.reshape(3 * CH, CH, 2, MX)[at].astype(FLT).reshape(2 * CH, MX)
@@ -385,12 +401,13 @@
         pool[:, 3] = jnp.zeros((6, 9, 2, HALF), BF)
 
     column = jnp.sum(t_spread_o[...].astype(FLT) * bias_in[...], axis=1, keepdims=True)
-    spot = lax.broadcasted_iota(jnp.int32, (40, HALF), 1)
+    spot = lax.broadcasted_iota(jnp.int32, (48, HALF), 1)
+    conv_matrix = conv[...].astype(BF)
     for pair in range(LX // 2):
-        sums = mm(conv[...], pool[pair : pair + 3].reshape(12 * CH, HALF))
-        below = jnp.where(spot >= STEPS, pltpu.roll(sums[0:40], STEPS, 1), 0.0)
-        above = jnp.where(spot < HALF - STEPS, pltpu.roll(sums[80:120], HALF - STEPS, 1), 0.0)
-        high, low = halves(jax.nn.gelu(sums[40:80] + below + above))
+        sums = mm(conv_matrix, pool[pair : pair + 3].reshape(12 * CH, HALF))
+        below = jnp.where(spot >= STEPS, pltpu.roll(sums[0:48], STEPS, 1), 0.0)
+        above = jnp.where(spot < HALF - STEPS, pltpu.roll(sums[96:144], HALF - STEPS, 1), 0.0)
+        high, low = halves(jax.nn.gelu(sums[48:96] + below + above))
         span = slice(pair * PAIR, (pair + 1) * PAIR)
         up = mm(t_row_up[...], mm(high, t_lane_up[...]).astype(BF))
         up = up + mm(t_row_up[...], mm(low, t_lane_up[...]).astype(BF))
@@ -473,7 +490,7 @@
     tables = make_tables()
     f = features.transpose(0, 2, 1, 3).reshape(LX * CH, LY, DEPTH)
     w = mode_weights.transpose(0, 1, 3, 4, 2, 5)
-    taps = conv_weight.reshape(3, 3, 3, CH, CH).transpose(2, 4, 0, 1, 3).reshape(3 * CH, 9 * CH)
+    taps = conv_weight.transpose(1, 2, 0)
     operands = [f, w, point_weight, bias_term.reshape(1, CH), taps]
     vmem = [
         pltpu.VMEM(f.shape, BF),
@@ -495,14 +512,15 @@
         pltpu.VMEM((GY, 4, ROWS), BF),
         pltpu.VMEM((6, 4, 9, 2, HALF), BF),
         pltpu.VMEM((PAIR, PAIR), BF),
-        pltpu.VMEM((120, 12 * CH), BF),
+        pltpu.VMEM((CH, 24, 128), FLT),
+        pltpu.VMEM((144, 12 * CH), FLT),
         pltpu.VMEM((3 * CH, 2 * CH, 128), FLT),
         pltpu.VMEM((6, SLOT, 128), FLT),
         pltpu.VMEM((6, SLOT, 128), FLT),
         pltpu.VMEM((ROWS, DEPTH), FLT),
         pltpu.VMEM(f.shape, BF),
         pltpu.SemaphoreType.DMA((5,)),
-        pltpu.SemaphoreType.DMA((16,)),
+        pltpu.SemaphoreType.DMA((TABLES,)),
         pltpu.SemaphoreType.DMA((4,)),
         pltpu.SemaphoreType.DMA((4,)),
         pltpu.SemaphoreType.DMA((4,)),
@@ -513,14 +531,14 @@
     out = pl.pallas_call(
         kernel,
         out_shape=jax.ShapeDtypeStruct(f.shape, BF),
-        in_specs=[pl.BlockSpec(memory_space=pl.ANY)] * (5 + len(tables)),
+        in_specs=[pl.BlockSpec(memory_space=pltpu.HBM)] * (5 + len(tables)),
         out_specs=pl.BlockSpec(memory_space=pl.ANY),
         scratch_shapes=vmem,
         compiler_params=pltpu.CompilerParams(
             collective_id=0, has_side_effects=True, vmem_limit_bytes=48 << 20
         ),
         name="layer",
-    )(*operands, *[jnp.asarray(t) for t in tables])
+    )(*[pltpu.with_memory_space_constraint(t, pltpu.HBM) for t in operands + [jnp.asarray(t) for t in tables]])
     return out.reshape(LX, CH, LY, DEPTH).transpose(0, 2, 1, 3)
 
 

time: 66.5 us -> 46.3 us (0.70)
  local copies, waits for them, and re-layouts: 19.2 us -> 0.82 us
  Pallas kernels: 46.5 us -> 45.3 us
    unnamed x40 -> x1, local copies, waits for them, and re-layouts: 18.7 us -> 0.82 us
    pallas_call x1, Pallas kernels: 46.5 us -> 45.3 us  [local(): pl.pallas_call(kernel, out_shape=jax.ShapeDtypeStruct(f.shape, BF), in_sp...]
where the time goes in v2:
time: 46.3 us; the launch traced here: 46.2 us
  Pallas kernels  45.3 us (98%)
  local copies, waits for them, and re-layouts  0.82 us (2%)
    pallas_call x1, Pallas kernels, local(): pl.pallas_call(kernel, out_shape=jax.ShapeDtypeStruct(f.shape, BF), in_sp...  45.3 us

profile of v2, /device:TPU:1, one launch (start us, length us, event | category | flops | bytes accessed | tf_op | source)
XLA Modules:
  0.0 46.2 jit_solution(7051287190628891280)
XLA Ops:
  0.0 45.3 %layer.1 = bf16[144,4,512]{2,1,0:T(4,128)(2,1)S(1)} custom-call(bf16[144,4,512]{2,1,0:T(4,128)(2,1)} %bitcast.11, bf16[2,24,18,18,2,24]{5,4,3,2,1,0:T(2,128)(2,1)} %bitcast.10, bf16[18,18]{1,0:T(8,128)(2,1)} %refs_2_.1, f32[1,18]{1,0:T(1,128)} %bitcast.13, bf16[18,18,27]{2,1,0:T(8,128)(2,1)} %bitcast.12, bf16[128,512]{1,0:T(8,128)(2,1)} %constant.34.clone.refs_5_, ...), custom_call_target="tpu_custom_call" | custom-call | tf_op jit(solution)/shard_map/layer/pallas_call | solution.py:531
  45.4 0.8 %copy.24 = bf16[8,4,18,512]{3,1,2,0:T(4,128)(2,1)} copy(bf16[8,4,18,512]{3,1,2,0:T(4,128)(2,1)S(1)} %bitcast.9) | data formatting | bytes 1179648

commit v3 on v2

--- a/solution.py
+++ b/solution.py
@@ -76,14 +76,11 @@
     zt_forward, zt_inverse = depth_tables()
     yf, yi = forward_table(MY, GY * LY), inverse_table(MY, GY * LY)
     xf, xi = forward_table(MX, GX * LX), inverse_table(MX, GX * LX)
-    eye2 = np.eye(2, dtype=np.float32)
     per = MY // 8
     block = yf.reshape(2, GY, LY, 2, 8, per)
-    ty = np.zeros((LY, 2, 8, JS, GY, 2, 2), np.float32)
-    ty[:, :, :, : 2 * per] = np.einsum("rgysaj,mn->ymajsgnr", block, eye2).reshape(
-        LY, 2, 8, 2 * per, GY, 2, 2
-    )
-    ty = ty.reshape(LY * GX * JS, GY * 4)
+    ty = np.zeros((LY, 8, JS, GY, 2), np.float32)
+    ty[:, :, : 2 * per] = np.einsum("rgysaj->yajsgr", block).reshape(LY, 8, 2 * per, GY, 2)
+    ty = ty.reshape(LY * 8 * JS, GY * 2)
     eyex, eyec, eyey = np.eye(LX), np.eye(CH, SLOT), np.eye(LY)
     gather = np.einsum("xX,cC,y->xcyXC", eyex, eyec, np.ones(LY)).reshape(ROWS, LX * SLOT)
     block = xf.reshape(2, GX, 2, 4, 2, MX)
@@ -100,11 +97,11 @@
     )
     tix = tix.reshape(GX * 2 * JS, per * 2 * 4 * SLOT)
     block = yi.reshape(2, 8, per, 2, GY, LY)
-    tiy = np.zeros((LY, GY, 2, 2, 2, 8, JS), np.float32)
-    tiy[..., : 2 * per] = np.einsum("rajsgy,mn->ygmsnajr", block, eye2).reshape(
-        LY, GY, 2, 2, 2, 8, 2 * per
-    )
-    tiy = tiy.reshape(LY * GY * 4, GX * JS)
+    tiy = np.zeros((LY, GY, 2, 8, JS), np.float32)
+    tiy[..., : 2 * per] = np.einsum("rajsgy->ygsajr", block).reshape(LY, GY, 2, 8, 2 * per)
+    tiy = tiy.reshape(LY * GY * 2, 8 * JS)
+    zt_forward = zt_forward.reshape(GY, 2, 2, DEPTH).transpose(1, 0, 2, 3).reshape(2 * MODES, DEPTH)
+    zt_inverse = zt_inverse.reshape(GY, 2, 2, DEPTH).transpose(1, 0, 2, 3).reshape(2, MODES, DEPTH)
     pair_pool = np.einsum("x,cC,yY->YCxcy", np.ones(2), np.eye(CH), np.repeat(np.eye(2), 2, 0))
     pair_pool = pair_pool.reshape(2 * CH, PAIR)
     lane_up = np.einsum("zZ,tT->ZTzt", np.repeat(np.eye(GRID_Z // 2), 2, 0), np.eye(STEPS))
@@ -196,7 +193,6 @@
         table_sem,
         send_sem,
         recv_sem,
-        own_sem,
         halo_send,
         halo_recv,
         out_sem,
@@ -228,15 +224,27 @@
         sign = 1 - 2 * lax.rem(step, 2)
         return count // 2 + sign * lax.div(step + 1, 2)
 
-    def on_gx(step):
-        x = lax.rem(lax.div(gx, 4) + far_first(lax.rem(step, 4), 4), 4)
-        y = lax.rem(lax.rem(gx, 4) + far_first(lax.div(step, 4), 4), 4)
-        return (4 * x + y, gy)
-
-    def on_gy(step):
-        z = lax.rem(lax.div(gy, 4) + far_first(lax.div(step, 4), 8), 8)
-        low = lax.rem(lax.rem(gy, 4) + far_first(lax.rem(step, 4), 4), 4)
-        return (gx, 4 * z + low)
+    far = (2, 1, 3, 0)
+    inner = lax.rem(gy, 4)
+    lows = [lax.rem(inner + k, 4) for k in far]
+    xs = [4 * lax.rem(lax.div(gx, 4) + k, 4) for k in far]
+
+    def each_gy(act):
+        def ring(step, _):
+            plane = 4 * lax.rem(lax.div(gy, 4) + far_first(step, 8), 8)
+            for k in range(4):
+                act(plane + lows[k])
+            return 0
+
+        lax.fori_loop(0, 7, ring, 0)
+        for k in range(3):
+            act(gy - inner + lows[k])
+
+    def each_gx(act):
+        for k in far:
+            y = lax.rem(lax.rem(gx, 4) + k, 4)
+            for i in range(4 if k else 3):
+                act(xs[i] + y)
 
     def greet(target):
         pl.semaphore_signal(barrier, inc=1, device_id=target, device_id_type=MESH)
@@ -256,16 +264,8 @@
     loads[0].start()
     mine[0].start()
 
-    def greet_gy(step, _):
-        greet(on_gy(step))
-        return 0
-
-    def greet_gx(step, _):
-        greet(on_gx(step))
-        return 0
-
-    lax.fori_loop(0, GY - 1, greet_gy, 0)
-    lax.fori_loop(0, GX - 1, greet_gx, 0)
+    each_gx(lambda to: greet((to, gy)))
+    each_gy(lambda to: greet((gx, to)))
     sides = [(dx, dy) for dx in (-1, 0, 1) for dy in (-1, 0, 1) if (dx, dy) != (0, 0)]
 
     def beside(dx, dy):
@@ -283,39 +283,35 @@
     loads[0].wait()
     f_rows[...] = f_in.reshape(ROWS, DEPTH)[...]
     hat = mm_nt(t_zf[...], f_rows[...]).astype(BF)
-    send_one[...] = hat.reshape(GY, 4, ROWS)
-
-    def all_to_all(at, count, source, target, me, place):
-        own = pltpu.make_async_copy(source.at[me], target.at[me], own_sem.at[at])
+    for m in range(2):
+        send_one[m] = hat[m * MODES : (m + 1) * MODES].reshape(GY, 2, ROWS)
+
+    def along_gy(at, source, target):
+        own = pltpu.make_async_copy(source.at[gy], target.at[gy], recv_sem.at[at])
         own.start()
 
-        def send(step, _):
-            to = place(step)
+        def send(to):
             pltpu.make_async_remote_copy(
-                src_ref=source.at[to[1] if count == GY else to[0]],
-                dst_ref=target.at[me],
+                src_ref=source.at[to],
+                dst_ref=target.at[gy],
                 send_sem=send_sem.at[at],
                 recv_sem=recv_sem.at[at],
-                device_id=to,
+                device_id=(gx, to),
                 device_id_type=MESH,
             ).start()
-            return 0
-
-        lax.fori_loop(0, count - 1, send, 0)
-
-        def arrive():
-            own.wait()
-            part = target.at[pl.ds(0, count - 1)]
-            pltpu.make_async_copy(part, part, recv_sem.at[at]).wait()
-
-        def leave():
-            part = source.at[pl.ds(0, count - 1)]
-            pltpu.make_async_copy(part, part, send_sem.at[at]).wait()
-
-        return arrive, leave
+
+        each_gy(send)
+
+    def arrived(at, whole):
+        pltpu.make_async_copy(whole, whole, recv_sem.at[at]).wait()
+
+    def left(at, source, count):
+        part = source.at[pl.ds(0, count)]
+        pltpu.make_async_copy(part, part, send_sem.at[at]).wait()
 
     pl.semaphore_wait(barrier, (GY - 1) + (GX - 1) + 4)
-    arrive_one, leave_one = all_to_all(0, GY, send_one, recv_one, gy, on_gy)
+    for m in range(2):
+        along_gy(m, send_one.at[m], recv_one.at[m])
 
     for i in (8, 9):
         loads[i].wait()
@@ -343,9 +339,104 @@
     for copy in rims:
         copy.start()
 
-    for i in range(1, 5):
+    mine[1].wait()
+
+    def widen(at, _):
+        w_wide[at, :, 0:MX] = w_in.reshape(3 * CH, CH, 2, MX)[at].astype(FLT).reshape(2 * CH, MX)
+        return 0
+
+    lax.fori_loop(0, 3 * CH, widen, 0)
+    mixed[...] = jnp.zeros_like(mixed)
+
+    for i in (1, 2):
+        loads[i].wait()
+    lane = lax.rem(lax.broadcasted_iota(jnp.int32, (8 * JS, ROWS), 1), LY)
+    for m in range(2):
+        arrived(m, recv_one.at[m])
+        part = mm(t_y[...], recv_one[m].reshape(2 * GY, ROWS)).reshape(LY, 8 * JS, ROWS)
+        chosen = part[0]
+        for y in range(1, LY):
+            chosen = jnp.where(lane == y, part[y], chosen)
+        both = mm(jnp.concatenate(halves(chosen), axis=0), t_gather[...])
+        second = both[: 8 * JS] + both[8 * JS :]
+        second = [second[:, h * 128 : (h + 1) * 128].reshape(8, JS, 128) for h in range(2)]
+        send_two[8 * m : 8 * m + 8] = jnp.concatenate(second, axis=1).astype(BF)
+
+        def send(step, _):
+            x = 2 * m + lax.rem(step, 2)
+            y = lax.rem(lax.rem(gx, 4) + far_first(lax.div(step, 2), 4), 4)
+            to = 4 * x + y
+
+            @pl.when(to != gx)
+            def _():
+                pltpu.make_async_remote_copy(
+                    src_ref=send_two.at[to],
+                    dst_ref=recv_two.at[gx],
+                    send_sem=send_sem.at[2],
+                    recv_sem=recv_sem.at[2],
+                    device_id=(to, gy),
+                    device_id_type=MESH,
+                ).start()
+
+            return 0
+
+        lax.fori_loop(0, 8, send, 0)
+    pltpu.make_async_copy(send_two.at[gx], recv_two.at[gx], recv_sem.at[2]).start()
+
+    for i in (3, 4):
+        loads[i].wait()
+    arrived(2, recv_two)
+    turned = mm_tn(recv_two[...].reshape(GX * 2 * JS, 128), t_x[...])
+    group = lax.broadcasted_iota(jnp.int32, (SLOT, 128), 1) // SLOT
+    for at in range(6):
+        acc = jnp.zeros((SLOT, 128), FLT)
+        for u in range(4):
+            piece = turned[u * SLOT : (u + 1) * SLOT, at * 128 : (at + 1) * 128]
+            acc = acc + jnp.where(group == u, piece, 0.0)
+        acc = acc + pltpu.roll(acc, 64, 1)
+        acc = acc + pltpu.roll(acc, 32, 1)
+        third[at] = acc
+
+    for j in range(3):
+        real = jnp.zeros((CH, 128), FLT)
+        imag = jnp.zeros((CH, 128), FLT)
+        for c in range(CH):
+            w_real = w_wide[j * CH + c, pl.ds(0, CH, stride=2), :]
+            w_imag = w_wide[j * CH + c, pl.ds(1, CH, stride=2), :]
+            u_real = third[2 * j, c : c + 1, :]
+            u_imag = third[2 * j + 1, c : c + 1, :]
+            real = real + (w_real * u_real - w_imag * u_imag)
+            imag = imag + (w_real * u_imag + w_imag * u_real)
+        mixed[2 * j, 0:CH, 0:MX] = real[:, 0:MX]
+        mixed[2 * j + 1, 0:CH, 0:MX] = imag[:, 0:MX]
+
+    blocks = []
+    for at in range(6):
+        value = mixed[at]
+        value = value + pltpu.roll(value, 32, 1)
+        value = value + pltpu.roll(value, 64, 1)
+        tall = [jnp.where(group == u, value, 0.0) for u in range(4)]
+        blocks.append(jnp.concatenate(tall, axis=0).astype(BF))
+    back = mm_nt(t_ix[...], jnp.concatenate(blocks, axis=1))
+    send_three[...] = back.astype(BF).reshape(GX, 2 * JS, 128)
+    at_three = 3 + lax.div(gx, 8)
+    pltpu.make_async_copy(send_three.at[gx], recv_three.at[gx], recv_sem.at[at_three]).start()
+
+    def send(to):
+        pltpu.make_async_remote_copy(
+            src_ref=send_three.at[to],
+            dst_ref=recv_three.at[gx],
+            send_sem=send_sem.at[3],
+            recv_sem=recv_sem.at[at_three],
+            device_id=(to, gy),
+            device_id_type=MESH,
+        ).start()
+
+    each_gx(send)
+
+    for i in (2, 3, 4):
         mine[i].wait()
-    for i in range(11, TABLES):
+    for i in range(10, TABLES):
         loads[i].wait()
     wide = mm_nt(t_spread_o[...], pw_in[...]).astype(BF)
     wide = mm_nt(wide, t_spread_o[...]).astype(BF)
@@ -358,29 +449,6 @@
         placed = mm(flat, t_conv_place[at]).astype(BF) * t_conv_same[...]
         conv[at * 24 : (at + 1) * 24] = mm(t_conv_sum[...], placed)
 
-    def widen(at, _):
-        w_wide[at, :, 0:MX] = w_in.reshape(3 * CH, CH, 2, MX)[at].astype(FLT).reshape(2 * CH, MX)
-        return 0
-
-    lax.fori_loop(0, 3 * CH, widen, 0)
-    mixed[...] = jnp.zeros_like(mixed)
-
-    for i in (1, 2):
-        loads[i].wait()
-    arrive_one()
-    lane = lax.broadcasted_iota(jnp.int32, (GX * JS, ROWS), 1)
-    part = mm(t_y[...], recv_one[...].reshape(4 * GY, ROWS)).reshape(LY, GX * JS, ROWS)
-    chosen = part[0]
-    for y in range(1, LY):
-        chosen = jnp.where(lax.rem(lane, LY) == y, part[y], chosen)
-    high, low = halves(chosen)
-    second = mm(high, t_gather[...]) + mm(low, t_gather[...])
-    second = [second[:, h * 128 : (h + 1) * 128].reshape(GX, JS, 128) for h in range(2)]
-    send_two[...] = jnp.concatenate(second, axis=1).astype(BF)
-    arrive_two, leave_two = all_to_all(1, GX, send_two, recv_two, gx, on_gx)
-
-    for i in (10,):
-        loads[i].wait()
     for copy in rims:
         copy.wait_recv()
 
@@ -399,6 +467,21 @@
     @pl.when(gy == GY - 1)
     def _():
         pool[:, 3] = jnp.zeros((6, 9, 2, HALF), BF)
+
+    for i in (5, 6, 7):
+        loads[i].wait()
+    for m in range(2):
+        mine_three = recv_three.at[pl.ds(8 * m, 8)]
+        arrived(3 + m, mine_three)
+        wide_in = mine_three[...].astype(FLT)
+        sides_in = [wide_in[:, h * JS : (h + 1) * JS].reshape(8 * JS, 128) for h in range(2)]
+        spread = mm(jnp.concatenate(sides_in, axis=1).astype(BF), t_spread[...]).astype(BF)
+        part = mm(t_iy[...], spread).reshape(LY, 2 * GY, ROWS)
+        chosen = part[0]
+        for y in range(1, LY):
+            chosen = jnp.where(lane == y, part[y], chosen)
+        send_four[m] = chosen.astype(BF).reshape(GY, 2, ROWS)
+        along_gy(5 + m, send_four.at[m], recv_four.at[m])
 
     column = jnp.sum(t_spread_o[...].astype(FLT) * bias_in[...], axis=1, keepdims=True)
     spot = lax.broadcasted_iota(jnp.int32, (48, HALF), 1)
@@ -413,77 +496,24 @@
         up = up + mm(t_row_up[...], mm(low, t_lane_up[...]).astype(BF))
         base[span] = mm(point[...], f_rows[span]) + up + column
 
-    for i in (3, 4):
-        loads[i].wait()
-    arrive_two()
-    turned = mm_tn(recv_two[...].reshape(GX * 2 * JS, 128), t_x[...])
-    group = lax.broadcasted_iota(jnp.int32, (SLOT, 128), 1) // SLOT
-    for at in range(6):
-        acc = jnp.zeros((SLOT, 128), FLT)
-        for u in range(4):
-            piece = turned[u * SLOT : (u + 1) * SLOT, at * 128 : (at + 1) * 128]
-            acc = acc + jnp.where(group == u, piece, 0.0)
-        acc = acc + pltpu.roll(acc, 64, 1)
-        acc = acc + pltpu.roll(acc, 32, 1)
-        third[at] = acc
-
-    for j in range(3):
-        real = jnp.zeros((CH, 128), FLT)
-        imag = jnp.zeros((CH, 128), FLT)
-        for c in range(CH):
-            w_real = w_wide[j * CH + c, pl.ds(0, CH, stride=2), :]
-            w_imag = w_wide[j * CH + c, pl.ds(1, CH, stride=2), :]
-            u_real = third[2 * j, c : c + 1, :]
-            u_imag = third[2 * j + 1, c : c + 1, :]
-            real = real + (w_real * u_real - w_imag * u_imag)
-            imag = imag + (w_real * u_imag + w_imag * u_real)
-        mixed[2 * j, 0:CH, 0:MX] = real[:, 0:MX]
-        mixed[2 * j + 1, 0:CH, 0:MX] = imag[:, 0:MX]
-
-    blocks = []
-    for at in range(6):
-        value = mixed[at]
-        value = value + pltpu.roll(value, 32, 1)
-        value = value + pltpu.roll(value, 64, 1)
-        tall = [jnp.where(group == u, value, 0.0) for u in range(4)]
-        blocks.append(jnp.concatenate(tall, axis=0).astype(BF))
-    back = mm_nt(t_ix[...], jnp.concatenate(blocks, axis=1))
-    send_three[...] = back.astype(BF).reshape(GX, 2 * JS, 128)
-    arrive_three, leave_three = all_to_all(2, GX, send_three, recv_three, gx, on_gx)
-
-    for i in (5, 6, 7):
-        loads[i].wait()
-    arrive_three()
-    wide_in = recv_three[...].astype(FLT)
-    sides_in = [wide_in[:, h * JS : (h + 1) * JS].reshape(GX * JS, 128) for h in range(2)]
-    spread = mm(jnp.concatenate(sides_in, axis=1).astype(BF), t_spread[...]).astype(BF)
-    part = mm(t_iy[...], spread).reshape(LY, 4 * GY, ROWS)
-    chosen = part[0]
-    for y in range(1, LY):
-        chosen = jnp.where(lax.rem(lane, LY) == y, part[y], chosen)
-    send_four[...] = chosen.astype(BF).reshape(GY, 4, ROWS)
-    arrive_four, leave_four = all_to_all(3, GY, send_four, recv_four, gy, on_gy)
-
-    arrive_four()
-    columns = recv_four[...].reshape(4 * GY, ROWS).astype(FLT).T.astype(BF)
-    stores = []
+    arrived(5, recv_four.at[0])
+    columns = recv_four[0].reshape(2 * GY, ROWS).astype(FLT).T.astype(BF)
     for pair in range(LX // 2):
         span = slice(pair * PAIR, (pair + 1) * PAIR)
-        total = mm(columns[span], t_zi[...]) + base[span]
-        out_rows[pair * 36 : (pair + 1) * 36] = jax.nn.gelu(total).astype(BF).reshape(36, 4, DEPTH)
-        store = pltpu.make_async_copy(
-            out_rows.at[pl.ds(pair * 36, 36)],
-            out_hbm.at[pl.ds(pair * 36, 36)],
-            out_sem.at[pair],
-        )
-        store.start()
-        stores.append(store)
-    for leave in (leave_one, leave_two, leave_three, leave_four):
-        leave()
+        base[span] += mm(columns[span], t_zi[0])
+    arrived(6, recv_four.at[1])
+    columns = recv_four[1].reshape(2 * GY, ROWS).astype(FLT).T.astype(BF)
+    for pair in range(LX // 2):
+        span = slice(pair * PAIR, (pair + 1) * PAIR)
+        total = mm(columns[span], t_zi[1]) + base[span]
+        out_hbm[pair * 36 : (pair + 1) * 36] = jax.nn.gelu(total).astype(BF).reshape(36, 4, DEPTH)
+    for m in range(2):
+        left(m, send_one.at[m], GY - 1)
+        left(5 + m, send_four.at[m], GY - 1)
+    left(2, send_two, GX - 1)
+    left(3, send_three, GX - 1)
     for copy in rims:
         copy.wait_send()
-    for store in stores:
-        store.wait()
 
 
 def local(features, mode_weights, point_weight, bias_term, conv_weight):
@@ -502,14 +532,14 @@
     vmem += [pltpu.VMEM(t.shape, BF) for t in tables]
     vmem += [
         pltpu.VMEM((ROWS, DEPTH), BF),
-        pltpu.VMEM((GY, 4, ROWS), BF),
-        pltpu.VMEM((GY, 4, ROWS), BF),
+        pltpu.VMEM((2, GY, 2, ROWS), BF),
+        pltpu.VMEM((2, GY, 2, ROWS), BF),
         pltpu.VMEM((GX, 2 * JS, 128), BF),
         pltpu.VMEM((GX, 2 * JS, 128), BF),
         pltpu.VMEM((GX, 2 * JS, 128), BF),
         pltpu.VMEM((GX, 2 * JS, 128), BF),
-        pltpu.VMEM((GY, 4, ROWS), BF),
-        pltpu.VMEM((GY, 4, ROWS), BF),
+        pltpu.VMEM((2, GY, 2, ROWS), BF),
+        pltpu.VMEM((2, GY, 2, ROWS), BF),
         pltpu.VMEM((6, 4, 9, 2, HALF), BF),
         pltpu.VMEM((PAIR, PAIR), BF),
         pltpu.VMEM((CH, 24, 128), FLT),
@@ -521,9 +551,8 @@
         pltpu.VMEM(f.shape, BF),
         pltpu.SemaphoreType.DMA((5,)),
         pltpu.SemaphoreType.DMA((TABLES,)),
-        pltpu.SemaphoreType.DMA((4,)),
-        pltpu.SemaphoreType.DMA((4,)),
-        pltpu.SemaphoreType.DMA((4,)),
+        pltpu.SemaphoreType.DMA((7,)),
+        pltpu.SemaphoreType.DMA((7,)),
         pltpu.SemaphoreType.DMA((8,)),
         pltpu.SemaphoreType.DMA((8,)),
         pltpu.SemaphoreType.DMA((4,)),
@@ -532,7 +561,7 @@
         kernel,
         out_shape=jax.ShapeDtypeStruct(f.shape, BF),
         in_specs=[pl.BlockSpec(memory_space=pltpu.HBM)] * (5 + len(tables)),
-        out_specs=pl.BlockSpec(memory_space=pl.ANY),
+        out_specs=pl.BlockSpec(memory_space=pltpu.VMEM),
         scratch_shapes=vmem,
         compiler_params=pltpu.CompilerParams(
             collective_id=0, has_side_effects=True, vmem_limit_bytes=48 << 20

time: 46.3 us -> 43.7 us (0.944)
  Pallas kernels: 45.3 us -> 42.8 us
    pallas_call x1, Pallas kernels: 45.3 us -> 42.8 us  [local(): pl.pallas_call(kernel, out_shape=jax.ShapeDtypeStruct(f.shape, BF), in_sp...]
where the time goes in v3:
time: 43.7 us; the launch traced here: 43.6 us
  Pallas kernels  42.8 us (98%)
  local copies, waits for them, and re-layouts  0.82 us (2%)
    pallas_call x1, Pallas kernels, local(): pl.pallas_call(kernel, out_shape=jax.ShapeDtypeStruct(f.shape, BF), in_sp...  42.8 us

profile of v3, /device:TPU:1, one launch (start us, length us, event | category | flops | bytes accessed | tf_op | source)
XLA Modules:
  0.0 43.6 jit_solution(4379790068681826321)
XLA Ops:
  0.0 42.8 %layer.1 = bf16[144,4,512]{2,1,0:T(4,128)(2,1)S(1)} custom-call(bf16[144,4,512]{2,1,0:T(4,128)(2,1)} %bitcast.11, bf16[2,24,18,18,2,24]{5,4,3,2,1,0:T(2,128)(2,1)} %bitcast.10, bf16[18,18]{1,0:T(8,128)(2,1)} %refs_2_.1, f32[1,18]{1,0:T(1,128)} %bitcast.13, bf16[18,18,27]{2,1,0:T(8,128)(2,1)} %bitcast.12, bf16[128,512]{1,0:T(8,128)(2,1)} %constant.34.clone.refs_5_, ...), custom_call_target="tpu_custom_call" | custom-call | tf_op jit(solution)/shard_map/layer/pallas_call | solution.py:560
  42.8 0.8 %copy.24 = bf16[8,4,18,512]{3,1,2,0:T(4,128)(2,1)} copy(bf16[8,4,18,512]{3,1,2,0:T(4,128)(2,1)S(1)} %bitcast.9) | data formatting | bytes 1179648

commit v4 on v3

--- a/solution.py
+++ b/solution.py
@@ -167,7 +167,7 @@
 def kernel(*refs):
     (f_hbm, w_hbm, pw_hbm, bias_hbm, cw_hbm), refs = refs[:5], refs[5:]
     tables_hbm, refs = refs[:TABLES], refs[TABLES:]
-    out_hbm, refs = refs[0], refs[1:]
+    out_ref, refs = refs[0], refs[1:]
     (f_in, w_in, pw_in, bias_in, cw_in), refs = refs[:5], refs[5:]
     tables, refs = refs[:TABLES], refs[TABLES:]
     (
@@ -186,16 +186,14 @@
         conv,
         w_wide,
         third,
-        mixed,
         base,
-        out_rows,
         in_sem,
         table_sem,
         send_sem,
         recv_sem,
         halo_send,
         halo_recv,
-        out_sem,
+        heard,
     ) = refs
     (
         t_zf,
@@ -220,23 +218,18 @@
     gy = lax.axis_index("gy")
     barrier = pltpu.get_barrier_semaphore()
 
-    def far_first(step, count):
-        sign = 1 - 2 * lax.rem(step, 2)
-        return count // 2 + sign * lax.div(step + 1, 2)
-
     far = (2, 1, 3, 0)
     inner = lax.rem(gy, 4)
     lows = [lax.rem(inner + k, 4) for k in far]
     xs = [4 * lax.rem(lax.div(gx, 4) + k, 4) for k in far]
 
+    planes = [4 * lax.rem(lax.div(gy, 4) + k, 8) for k in range(1, 8)]
+
     def each_gy(act):
-        def ring(step, _):
-            plane = 4 * lax.rem(lax.div(gy, 4) + far_first(step, 8), 8)
+        for step in (4, 3, 5, 2, 6, 1, 7):
+            plane = planes[step - 1]
             for k in range(4):
                 act(plane + lows[k])
-            return 0
-
-        lax.fori_loop(0, 7, ring, 0)
         for k in range(3):
             act(gy - inner + lows[k])
 
@@ -264,7 +257,12 @@
     loads[0].start()
     mine[0].start()
 
-    each_gx(lambda to: greet((to, gy)))
+    at_y = lax.rem(gx, 4)
+    x_mates = [xs[i] + at_y for i in range(3)]
+    for mate in x_mates:
+        greet((mate, gy))
+    for k in (2, 1, 3):
+        greet((gx - at_y + lax.rem(at_y + k, 4), gy))
     each_gy(lambda to: greet((gx, to)))
     sides = [(dx, dy) for dx in (-1, 0, 1) for dy in (-1, 0, 1) if (dx, dy) != (0, 0)]
 
@@ -309,9 +307,11 @@
         part = source.at[pl.ds(0, count)]
         pltpu.make_async_copy(part, part, send_sem.at[at]).wait()
 
-    pl.semaphore_wait(barrier, (GY - 1) + (GX - 1) + 4)
+    pl.semaphore_wait(barrier, (GY - 1) + 6 + 4)
     for m in range(2):
         along_gy(m, send_one.at[m], recv_one.at[m])
+    for mate in x_mates:
+        pl.semaphore_signal(heard, inc=1, device_id=(mate, gy), device_id_type=MESH)
 
     for i in (8, 9):
         loads[i].wait()
@@ -336,17 +336,17 @@
         )
 
     rims = [rim(i, dx, dy) for i, (dx, dy) in enumerate(sides)]
-    for copy in rims:
-        copy.start()
-
+
+    w_wide[...] = jnp.zeros_like(w_wide)
     mine[1].wait()
 
     def widen(at, _):
-        w_wide[at, :, 0:MX] = w_in.reshape(3 * CH, CH, 2, MX)[at].astype(FLT).reshape(2 * CH, MX)
+        value = w_in.reshape(3 * CH, CH, 2, MX)[at].astype(FLT).reshape(2 * CH, MX)
+        for u in range(4):
+            w_wide[at, 0 : 2 * CH, u * SLOT : u * SLOT + MX] = value
         return 0
 
     lax.fori_loop(0, 3 * CH, widen, 0)
-    mixed[...] = jnp.zeros_like(mixed)
 
     for i in (1, 2):
         loads[i].wait()
@@ -362,26 +362,27 @@
         second = [second[:, h * 128 : (h + 1) * 128].reshape(8, JS, 128) for h in range(2)]
         send_two[8 * m : 8 * m + 8] = jnp.concatenate(second, axis=1).astype(BF)
 
-        def send(step, _):
-            x = 2 * m + lax.rem(step, 2)
-            y = lax.rem(lax.rem(gx, 4) + far_first(lax.div(step, 2), 4), 4)
-            to = 4 * x + y
-
-            @pl.when(to != gx)
-            def _():
-                pltpu.make_async_remote_copy(
-                    src_ref=send_two.at[to],
-                    dst_ref=recv_two.at[gx],
-                    send_sem=send_sem.at[2],
-                    recv_sem=recv_sem.at[2],
-                    device_id=(to, gy),
-                    device_id_type=MESH,
-                ).start()
-
-            return 0
-
-        lax.fori_loop(0, 8, send, 0)
+        if m == 0:
+            pl.semaphore_wait(heard, 3)
+        for k in far:
+            y = lax.rem(lax.rem(gx, 4) + k, 4)
+            for x in (2 * m, 2 * m + 1):
+                to = 4 * x + y
+
+                @pl.when(to != gx)
+                def _(to=to):
+                    pltpu.make_async_remote_copy(
+                        src_ref=send_two.at[to],
+                        dst_ref=recv_two.at[gx],
+                        send_sem=send_sem.at[2],
+                        recv_sem=recv_sem.at[2],
+                        device_id=(to, gy),
+                        device_id_type=MESH,
+                    ).start()
+
     pltpu.make_async_copy(send_two.at[gx], recv_two.at[gx], recv_sem.at[2]).start()
+    for copy in rims:
+        copy.start()
 
     for i in (3, 4):
         loads[i].wait()
@@ -397,26 +398,22 @@
         acc = acc + pltpu.roll(acc, 32, 1)
         third[at] = acc
 
+    blocks = []
     for j in range(3):
-        real = jnp.zeros((CH, 128), FLT)
-        imag = jnp.zeros((CH, 128), FLT)
+        real = jnp.zeros((24, 128), FLT)
+        imag = jnp.zeros((24, 128), FLT)
         for c in range(CH):
-            w_real = w_wide[j * CH + c, pl.ds(0, CH, stride=2), :]
-            w_imag = w_wide[j * CH + c, pl.ds(1, CH, stride=2), :]
+            w_real = w_wide[j * CH + c, pl.ds(0, 24, stride=2), :]
+            w_imag = w_wide[j * CH + c, pl.ds(1, 24, stride=2), :]
             u_real = third[2 * j, c : c + 1, :]
             u_imag = third[2 * j + 1, c : c + 1, :]
             real = real + (w_real * u_real - w_imag * u_imag)
             imag = imag + (w_real * u_imag + w_imag * u_real)
-        mixed[2 * j, 0:CH, 0:MX] = real[:, 0:MX]
-        mixed[2 * j + 1, 0:CH, 0:MX] = imag[:, 0:MX]
-
-    blocks = []
-    for at in range(6):
-        value = mixed[at]
-        value = value + pltpu.roll(value, 32, 1)
-        value = value + pltpu.roll(value, 64, 1)
-        tall = [jnp.where(group == u, value, 0.0) for u in range(4)]
-        blocks.append(jnp.concatenate(tall, axis=0).astype(BF))
+        for value in (real, imag):
+            tall = []
+            for u in range(4):
+                tall += [jnp.where(group[:24] == u, value, 0.0), jnp.zeros((8, 128), FLT)]
+            blocks.append(jnp.concatenate(tall, axis=0).astype(BF))
     back = mm_nt(t_ix[...], jnp.concatenate(blocks, axis=1))
     send_three[...] = back.astype(BF).reshape(GX, 2 * JS, 128)
     at_three = 3 + lax.div(gx, 8)
@@ -506,7 +503,7 @@
     for pair in range(LX // 2):
         span = slice(pair * PAIR, (pair + 1) * PAIR)
         total = mm(columns[span], t_zi[1]) + base[span]
-        out_hbm[pair * 36 : (pair + 1) * 36] = jax.nn.gelu(total).astype(BF).reshape(36, 4, DEPTH)
+        out_ref[pair * 36 : (pair + 1) * 36] = jax.nn.gelu(total).astype(BF).reshape(36, 4, DEPTH)
     for m in range(2):
         left(m, send_one.at[m], GY - 1)
         left(5 + m, send_four.at[m], GY - 1)
@@ -544,18 +541,16 @@
         pltpu.VMEM((PAIR, PAIR), BF),
         pltpu.VMEM((CH, 24, 128), FLT),
         pltpu.VMEM((144, 12 * CH), FLT),
-        pltpu.VMEM((3 * CH, 2 * CH, 128), FLT),
-        pltpu.VMEM((6, SLOT, 128), FLT),
+        pltpu.VMEM((3 * CH, 48, 128), FLT),
         pltpu.VMEM((6, SLOT, 128), FLT),
         pltpu.VMEM((ROWS, DEPTH), FLT),
-        pltpu.VMEM(f.shape, BF),
         pltpu.SemaphoreType.DMA((5,)),
         pltpu.SemaphoreType.DMA((TABLES,)),
         pltpu.SemaphoreType.DMA((7,)),
         pltpu.SemaphoreType.DMA((7,)),
         pltpu.SemaphoreType.DMA((8,)),
         pltpu.SemaphoreType.DMA((8,)),
-        pltpu.SemaphoreType.DMA((4,)),
+        pltpu.SemaphoreType.REGULAR,
     ]
     out = pl.pallas_call(
         kernel,

time: 43.7 us -> 42.5 us (0.973)
  Pallas kernels: 42.8 us -> 41.5 us
    pallas_call x1, Pallas kernels: 42.8 us -> 41.5 us  [local(): pl.pallas_call(kernel, out_shape=jax.ShapeDtypeStruct(f.shape, BF), in_sp...]
where the time goes in v4:
time: 42.5 us; the launch traced here: 42.4 us
  Pallas kernels  41.5 us (98%)
  local copies, waits for them, and re-layouts  0.82 us (2%)
    pallas_call x1, Pallas kernels, local(): pl.pallas_call(kernel, out_shape=jax.ShapeDtypeStruct(f.shape, BF), in_sp...  41.5 us

profile of v4, /device:TPU:1, one launch (start us, length us, event | category | flops | bytes accessed | tf_op | source)
XLA Modules:
  0.0 42.4 jit_solution(3274349131803640440)
XLA Ops:
  0.0 41.5 %layer.1 = bf16[144,4,512]{2,1,0:T(4,128)(2,1)S(1)} custom-call(bf16[144,4,512]{2,1,0:T(4,128)(2,1)} %bitcast.11, bf16[2,24,18,18,2,24]{5,4,3,2,1,0:T(2,128)(2,1)} %bitcast.10, bf16[18,18]{1,0:T(8,128)(2,1)} %refs_2_.1, f32[1,18]{1,0:T(1,128)} %bitcast.13, bf16[18,18,27]{2,1,0:T(8,128)(2,1)} %bitcast.12, bf16[128,512]{1,0:T(8,128)(2,1)} %constant.34.clone.refs_5_, ...), custom_call_target="tpu_custom_call" | custom-call | tf_op jit(solution)/shard_map/layer/pallas_call | solution.py:555
  41.6 0.8 %copy.24 = bf16[8,4,18,512]{3,1,2,0:T(4,128)(2,1)} copy(bf16[8,4,18,512]{3,1,2,0:T(4,128)(2,1)S(1)} %bitcast.9) | data formatting | bytes 1179648

commit v5 on v4

--- a/solution.py
+++ b/solution.py
@@ -257,13 +257,13 @@
     loads[0].start()
     mine[0].start()
 
+    each_gy(lambda to: greet((gx, to)))
     at_y = lax.rem(gx, 4)
     x_mates = [xs[i] + at_y for i in range(3)]
     for mate in x_mates:
         greet((mate, gy))
     for k in (2, 1, 3):
         greet((gx - at_y + lax.rem(at_y + k, 4), gy))
-    each_gy(lambda to: greet((gx, to)))
     sides = [(dx, dy) for dx in (-1, 0, 1) for dy in (-1, 0, 1) if (dx, dy) != (0, 0)]
 
     def beside(dx, dy):
@@ -312,14 +312,6 @@
         along_gy(m, send_one.at[m], recv_one.at[m])
     for mate in x_mates:
         pl.semaphore_signal(heard, inc=1, device_id=(mate, gy), device_id_type=MESH)
-
-    for i in (8, 9):
-        loads[i].wait()
-    for pair in range(LX // 2):
-        rows = mm(t_pair_pool[...], f_rows[pair * PAIR : (pair + 1) * PAIR])
-        high, low = halves(rows)
-        cells = mm(high, t_lane_pool[...]) + mm(low, t_lane_pool[...])
-        pool[pair + 1, 1:3] = cells.astype(BF).reshape(2, 9, 2, HALF)
 
     def rim(which, dx, dy):
         sx = {-1: pl.ds(1, 1), 0: pl.ds(1, 4), 1: pl.ds(4, 1)}[dx]
@@ -381,6 +373,14 @@
                     ).start()
 
     pltpu.make_async_copy(send_two.at[gx], recv_two.at[gx], recv_sem.at[2]).start()
+    for i in (8, 9):
+        loads[i].wait()
+    for pair in range(LX // 2):
+        rows = mm(t_pair_pool[...], f_rows[pair * PAIR : (pair + 1) * PAIR])
+        high, low = halves(rows)
+        cells = mm(high, t_lane_pool[...]) + mm(low, t_lane_pool[...])
+        pool[pair + 1, 1:3] = cells.astype(BF).reshape(2, 9, 2, HALF)
+
     for copy in rims:
         copy.start()
 

time: 42.5 us -> 42 us (0.988)
    pallas_call x1, Pallas kernels: 41.5 us -> 41.1 us  [local(): pl.pallas_call(kernel, out_shape=jax.ShapeDtypeStruct(f.shape, BF), in_sp...]
where the time goes in v5:
time: 42 us; the launch traced here: 41.9 us
  Pallas kernels  41.1 us (98%)
  local copies, waits for them, and re-layouts  0.82 us (2%)
    pallas_call x1, Pallas kernels, local(): pl.pallas_call(kernel, out_shape=jax.ShapeDtypeStruct(f.shape, BF), in_sp...  41.1 us

profile of v5, /device:TPU:1, one launch (start us, length us, event | category | flops | bytes accessed | tf_op | source)
XLA Modules:
  0.0 41.9 jit_solution(5685108199521807314)
XLA Ops:
  0.0 41.1 %layer.1 = bf16[144,4,512]{2,1,0:T(4,128)(2,1)S(1)} custom-call(bf16[144,4,512]{2,1,0:T(4,128)(2,1)} %bitcast.11, bf16[2,24,18,18,2,24]{5,4,3,2,1,0:T(2,128)(2,1)} %bitcast.10, bf16[18,18]{1,0:T(8,128)(2,1)} %refs_2_.1, f32[1,18]{1,0:T(1,128)} %bitcast.13, bf16[18,18,27]{2,1,0:T(8,128)(2,1)} %bitcast.12, bf16[128,512]{1,0:T(8,128)(2,1)} %constant.34.clone.refs_5_, ...), custom_call_target="tpu_custom_call" | custom-call | tf_op jit(solution)/shard_map/layer/pallas_call | solution.py:555
  41.1 0.8 %copy.24 = bf16[8,4,18,512]{3,1,2,0:T(4,128)(2,1)} copy(bf16[8,4,18,512]{3,1,2,0:T(4,128)(2,1)S(1)} %bitcast.9) | data formatting | bytes 1179648

commit v6 on v5

--- a/solution.py
+++ b/solution.py
@@ -285,9 +285,6 @@
         send_one[m] = hat[m * MODES : (m + 1) * MODES].reshape(GY, 2, ROWS)
 
     def along_gy(at, source, target):
-        own = pltpu.make_async_copy(source.at[gy], target.at[gy], recv_sem.at[at])
-        own.start()
-
         def send(to):
             pltpu.make_async_remote_copy(
                 src_ref=source.at[to],
@@ -299,6 +296,7 @@
             ).start()
 
         each_gy(send)
+        pltpu.make_async_copy(source.at[gy], target.at[gy], recv_sem.at[at]).start()
 
     def arrived(at, whole):
         pltpu.make_async_copy(whole, whole, recv_sem.at[at]).wait()
@@ -417,7 +415,6 @@
     back = mm_nt(t_ix[...], jnp.concatenate(blocks, axis=1))
     send_three[...] = back.astype(BF).reshape(GX, 2 * JS, 128)
     at_three = 3 + lax.div(gx, 8)
-    pltpu.make_async_copy(send_three.at[gx], recv_three.at[gx], recv_sem.at[at_three]).start()
 
     def send(to):
         pltpu.make_async_remote_copy(
@@ -430,6 +427,7 @@
         ).start()
 
     each_gx(send)
+    pltpu.make_async_copy(send_three.at[gx], recv_three.at[gx], recv_sem.at[at_three]).start()
 
     for i in (2, 3, 4):
         mine[i].wait()

time: 42 us -> 42 us (level)
  no operation moved by 1% of the time
where the time goes in v6:
time: 42 us; the launch traced here: 41.9 us
  Pallas kernels  41.1 us (98%)
  local copies, waits for them, and re-layouts  0.82 us (2%)
    pallas_call x1, Pallas kernels, local(): pl.pallas_call(kernel, out_shape=jax.ShapeDtypeStruct(f.shape, BF), in_sp...  41.1 us

profile of v6, /device:TPU:1, one launch (start us, length us, event | category | flops | bytes accessed | tf_op | source)
XLA Modules:
  0.0 41.9 jit_solution(7197190926692311306)
XLA Ops:
  0.0 41.1 %layer.1 = bf16[144,4,512]{2,1,0:T(4,128)(2,1)S(1)} custom-call(bf16[144,4,512]{2,1,0:T(4,128)(2,1)} %bitcast.11, bf16[2,24,18,18,2,24]{5,4,3,2,1,0:T(2,128)(2,1)} %bitcast.10, bf16[18,18]{1,0:T(8,128)(2,1)} %refs_2_.1, f32[1,18]{1,0:T(1,128)} %bitcast.13, bf16[18,18,27]{2,1,0:T(8,128)(2,1)} %bitcast.12, bf16[128,512]{1,0:T(8,128)(2,1)} %constant.34.clone.refs_5_, ...), custom_call_target="tpu_custom_call" | custom-call | tf_op jit(solution)/shard_map/layer/pallas_call | solution.py:553
  41.1 0.8 %copy.24 = bf16[8,4,18,512]{3,1,2,0:T(4,128)(2,1)} copy(bf16[8,4,18,512]{3,1,2,0:T(4,128)(2,1)S(1)} %bitcast.9) | data formatting | bytes 1179648
